TPU v7x, 32 devices: a whole 2x2x4 slice. The times are simulated.
32 devices in a mesh: ctx: 8 (over z, x), ch: 4 (over y, core).
Axes of the slice: x: 2, y: 2, z: 4, core: 2. Of those that a mesh axis runs over, the one named last changes fastest.
Arguments:
- tokens: bfloat16 [2048, 8192], P('ctx', 'ch'), may hold values from -6 to 6
- in_weight: bfloat16 [8192, 3, 8192], P('ctx', None, 'ch'), may hold values from -0.0625 to 0.0625
- short_filter: bfloat16 [3, 3, 8192], P(None, None, 'ch'), may hold values from -3 to 3
- decay_rate: float32 [8192, 16], P('ch'), may hold values from 2.4414063e-05 to 0.0333333333
- residue: float32 [8192, 16], P('ch'), may hold values from -0.12 to 0.12
- skip_gain: float32 [8192], P('ch'), may hold values from -4 to 4
Outputs:
- filtered: bfloat16 [2048, 8192], P('ctx', 'ch')
All inputs are finite; a program needn't handle non-finite values.
Results may differ from a plain program's by a relative error of at most 0.007.
Values may be sent and summed in bfloat16 or wider, within the bound.
A program may use at most 128 MiB of HBM per device.

v0:
```python
import jax
import jax.numpy as jnp
from jax import lax
from jax.experimental import pallas as pl
from jax.experimental.pallas import tpu as pltpu
from jax.sharding import PartitionSpec as P

LINE = 4
CORES = 2
VMEM_LIMIT = 40 * 1024 * 1024
STEPS = 8


def state_kernel(gated_ref, keep_ref, state_ref):
    modes = keep_ref.shape[0]

    def body(i, state):
        for u in range(STEPS):
            row = gated_ref[i * STEPS + u]
            state = tuple(keep_ref[m] * state[m] + row for m in range(modes))
        return state

    zero = jnp.zeros(keep_ref.shape[1:], jnp.float32)
    state = lax.fori_loop(0, gated_ref.shape[0] // STEPS, body, (zero,) * modes)
    for m in range(modes):
        state_ref[m] = state[m]


def mix_kernel(gated_ref, query_ref, keep_ref, residue_ref, skip_ref, enter_ref, out_ref):
    modes = keep_ref.shape[0]

    def body(i, state):
        for u in range(STEPS):
            t = i * STEPS + u
            row = gated_ref[t]
            state = tuple(keep_ref[m] * state[m] + row for m in range(modes))
            terms = [residue_ref[m] * state[m] for m in range(modes)]
            terms.append(skip_ref[...] * row)
            while len(terms) > 1:
                terms = [sum(terms[k : k + 2][1:], terms[k]) for k in range(0, len(terms), 2)]
            out_ref[t] = query_ref[t] * terms[0]
        return state

    start = tuple(enter_ref[m] for m in range(modes))
    lax.fori_loop(0, gated_ref.shape[0] // STEPS, body, start)


def rolled(array, x, feats, n_x):
    result = array
    for k in range(1, n_x):
        result = jnp.where(x == k, jnp.roll(array, -k * feats, axis=-1), result)
    return result


def call(kernel, out_shape, count):
    return pl.pallas_call(
        kernel,
        out_shape=jax.ShapeDtypeStruct(out_shape, jnp.float32),
        in_specs=[pl.BlockSpec(memory_space=pltpu.VMEM)] * count,
        out_specs=pl.BlockSpec(memory_space=pltpu.VMEM),
        compiler_params=pltpu.CompilerParams(vmem_limit_bytes=VMEM_LIMIT),
    )


def local(tokens, in_weight, short_filter, decay_rate, residue, skip_gain):
    n_ctx, n_ch = lax.axis_size("ctx"), lax.axis_size("ch")
    n_x = n_ctx // LINE
    n_q = n_ch // LINE
    me = lax.axis_index("ctx")
    z, x = me // n_x, me % n_x
    tok_rows = tokens.shape[0]
    feats, streams, width = in_weight.shape
    part = width // n_x
    rows = tok_rows * n_x
    modes = decay_rate.shape[1]

    def along_z(block, hop):
        route = [
            (i * n_x + k, (i + hop) * n_x + k)
            for i in range(LINE)
            if 0 <= i + hop < LINE
            for k in range(n_x)
        ]
        return lax.ppermute(block, "ctx", route)

    def along_x(block, hop):
        route = [
            (i * n_x + k, i * n_x + (k + hop) % n_x) for i in range(LINE) for k in range(n_x)
        ]
        return lax.ppermute(block, "ctx", route)

    def weight_part(g, index):
        return lax.dynamic_slice_in_dim(in_weight[:, g], index * part, part, axis=1)

    away = [[weight_part(g, (x + hop) % n_x) for hop in range(1, n_x)] for g in range(streams)]

    def exchange(g):
        return [along_x(block, hop) for hop, block in enumerate(away[g], 1)]

    route = [
        ((i * n_x + k) * n_ch + a * n_q + q, (a * n_x + k) * n_ch + i * n_q + q)
        for i in range(LINE)
        for k in range(n_x)
        for a in range(LINE)
        for q in range(n_q)
    ]
    moved = lax.ppermute(tokens, ("ctx", "ch"), route)
    moved, away[0] = lax.optimization_barrier((moved, away[0]))
    came = [exchange(0)]
    beside = [along_x(moved, hop) if hop else moved for hop in range(n_x)]
    if n_q == 1:
        beside = [rolled(block, x, feats, n_x) for block in beside]

    mine = lax.axis_index("ch")
    outer = n_ch // CORES

    def along_outer(block, hop):
        route = [(i, (i + hop * CORES) % n_ch) for i in range(n_ch)]
        return lax.ppermute(block, "ch", route)

    def other_core(block):
        return lax.ppermute(block, "ch", [(i, i ^ 1) for i in range(n_ch)])

    found = jnp.zeros((n_ch, n_x) + moved.shape, moved.dtype)
    for hop in range(n_x):
        for step in range(outer):
            block = along_outer(beside[hop], step) if step else beside[hop]
            source = (mine - step * CORES) % n_ch
            for core, piece in enumerate((block, other_core(block))):
                owner = source + core * (1 - 2 * (mine % CORES))
                found = lax.dynamic_update_slice(
                    found, piece[None, None], (owner, (x - hop) % n_x, 0, 0)
                )
    beside, away[1:] = lax.optimization_barrier((beside, away[1:]))
    came += [exchange(g) for g in range(1, streams)]
    found = found.reshape(LINE, n_q, n_x, tok_rows, tokens.shape[1])
    plane = found.transpose(0, 2, 3, 1, 4).reshape(LINE, rows, n_x * feats)
    if n_q > 1:
        plane = rolled(plane, x, feats, n_x)

    weights = [
        jnp.concatenate([weight_part(g, x)] + came[g][::-1], axis=0) for g in range(streams)
    ]

    def share(g, index, source):
        block = lax.dynamic_index_in_dim(source, index, 0, keepdims=False)
        return jnp.dot(block, weights[g], preferred_element_type=jnp.float32)

    def choose(values):
        return sum(jnp.where(z == i, value, 0) for i, value in enumerate(values))

    def hops(block, pairs):
        return lax.ppermute(
            block, "ctx", [(i * n_x + k, j * n_x + k) for i, j in pairs for k in range(n_x)]
        )

    first = choose([3, 3, 0, 0])
    second = choose([2, 3, 0, 1])
    third_up = choose([1, 2, 3, 3])
    third_down = choose([0, 0, 1, 2])
    low, wide = jnp.bfloat16, jnp.float32

    def reduce_stream(g):
        one = hops(share(g, first, plane).astype(low), [(0, 1), (3, 2)])
        two = (share(g, second, plane) + one.astype(wide)).astype(low)
        two, later = lax.optimization_barrier((two, plane))
        up, down = hops(two, [(0, 1), (1, 2)]), hops(two, [(3, 2), (2, 1)])
        up = (share(g, third_up, later) + up.astype(wide)).astype(low)
        down = (share(g, third_down, later) + down.astype(wide)).astype(low)
        up, down, later = lax.optimization_barrier((up, down, later))
        up, down = hops(up, [(0, 1), (1, 2), (2, 3)]), hops(down, [(3, 2), (2, 1), (1, 0)])
        return share(g, z, later) + up.astype(wide) + down.astype(wide)

    taps = lax.dynamic_slice_in_dim(short_filter, x * part, part, axis=2).astype(jnp.float32)
    tap_count = taps.shape[0]
    projected = [reduce_stream(g) for g in range(streams)]
    halo = along_z(jnp.stack([sums[rows - (tap_count - 1) :] for sums in projected]), 1)
    featured = []
    for g in range(streams):
        padded = jnp.concatenate([halo[g], projected[g]], axis=0)
        total = jnp.zeros((rows, part), jnp.float32)
        for back in range(tap_count):
            begin = tap_count - 1 - back
            total = total + taps[back, g][None] * padded[begin : begin + rows]
        featured.append(total)

    lanes = 128
    tile = (part // lanes, lanes)
    query = featured[0].reshape((rows,) + tile)
    gated = (featured[1] * featured[2]).reshape((rows,) + tile)

    def by_mode(array):
        mine = lax.dynamic_slice_in_dim(array, x * part, part, axis=0)
        return mine.T.reshape((modes,) + tile)

    rate, weight = by_mode(decay_rate), by_mode(residue)
    skip = lax.dynamic_slice_in_dim(skip_gain, x * part, part, axis=0).reshape(tile)
    keep = jnp.exp(-rate)
    state = call(state_kernel, (modes,) + tile, 2)(gated, keep)
    enter = jnp.zeros_like(state)
    for hop in range(1, LINE):
        enter = enter + along_z(state, hop) * jnp.exp(-rate * float((hop - 1) * rows))
    mixed = call(mix_kernel, (rows,) + tile, 6)(gated, query, keep, weight, skip, enter)
    mixed = mixed.reshape(n_x, tok_rows, part).astype(jnp.bfloat16)

    out = jnp.zeros((tok_rows, width), jnp.bfloat16)
    for hop in range(n_x):
        block = lax.dynamic_index_in_dim(mixed, (x + hop) % n_x, 0, keepdims=False)
        if hop:
            block = along_x(block, hop)
        out = lax.dynamic_update_slice_in_dim(out, block, ((x - hop) % n_x) * part, axis=1)
    return out


def solution(mesh):
    in_specs = (
        P("ctx", "ch"),
        P("ctx", None, "ch"),
        P(None, None, "ch"),
        P("ch", None),
        P("ch", None),
        P("ch"),
    )
    out_specs = P("ctx", "ch")
    return jax.shard_map(local, mesh=mesh, in_specs=in_specs, out_specs=out_specs, check_vma=False)
```

profile of v0, /device:TPU:0, one launch (start us, length us, event | category | flops | bytes accessed | tf_op | source)
XLA Modules:
  0.0 439.5 jit_solution(11305550853652191572)
XLA Ops:
  0.0 2.0 collective-permute-start
  2.0 7.8 %fusion.107 = (bf16[1024,1,2048]{2,0,1:T(8,128)(2,1)}, bf16[1024,1,2048]{2,0,1:T(8,128)(2,1)S(1)}, bf16[1024,1,2048]{2,0,1:T(8,128)(2,1)}) fusion(bf16[1024,3,2048]{2,0,1:T(8,128)(2,1)} %param.7), kind=kLoop, calls=%fused_computation.144 | loop fusion | bytes 25165824 | tf_op jit(solution)/shard_map/slice | solution.py:93
  9.8 2.5 dynamic-slice_bitcast_fusion.1
  12.4 4.4 broadcast_in_dim.31
  16.7 1.5 bitcast_dynamic-update-slice_fusion.7
  18.2 42.9 %collective-permute-start.2 = (bf16[256,2048]{1,0:T(8,128)(2,1)S(1)}, bf16[256,2048]{1,0:T(8,128)(2,1)}, u32[]{:S(2)}, u32[]{:S(2)}) collective-permute-start(bf16[256,2048]{1,0:T(8,128)(2,1)S(1)} %get-tuple-element.46), channel_id=1, source_target_pairs={{0,2},{1,3},{2,0},{3,1},{4,6},{5,7},{6,4},{7,5},{8,10},{9,11},{10,... | collective-permute-start | bytes 3145736 | tf_op jit(solution)/shard_map/ppermute | solution.py:119
  61.1 1.5 collective-permute-start.4
  62.6 11.4 %collective-permute-done.2 = bf16[256,2048]{1,0:T(8,128)(2,1)} collective-permute-done((bf16[256,2048]{1,0:T(8,128)(2,1)S(1)}, bf16[256,2048]{1,0:T(8,128)(2,1)}, u32[]{:S(2)}, u32[]{:S(2)}) %collective-permute-start.2) | collective-permute-done | bytes 1048608 | tf_op jit(solution)/shard_map/ppermute | solution.py:119
  74.0 1.9 collective-permute-done.4
  76.0 2.3 bitcast_dynamic-update-slice_fusion.6
  78.3 2.5 bitcast_dynamic-update-slice_fusion.5
  81.8 1.5 bitcast_dynamic-update-slice_fusion.3
  83.7 1.4 collective-permute-start.14
  85.1 2.8 dynamic-slice_bitcast_fusion
  87.9 19.5 %collective-permute-done.6 = bf16[256,2048]{1,0:T(8,128)(2,1)} collective-permute-done((bf16[256,2048]{1,0:T(8,128)(2,1)S(1)}, bf16[256,2048]{1,0:T(8,128)(2,1)}, u32[]{:S(2)}, u32[]{:S(2)}) %collective-permute-start.6) | collective-permute-done | bytes 1048608 | tf_op jit(solution)/shard_map/ppermute | solution.py:119
  107.5 1.5 collective-permute-start.8
  109.6 2.3 bitcast_dynamic-update-slice_fusion.2
  111.9 2.5 bitcast_dynamic-update-slice_fusion.1
  114.4 2.4 bitcast_dynamic-update-slice_fusion
  116.7 15.8 %collective-permute-done.14 = bf16[1024,1024]{1,0:T(8,128)(2,1)} collective-permute-done((bf16[1024,1024]{1,0:T(8,128)(2,1)}, bf16[1024,1024]{1,0:T(8,128)(2,1)}, u32[]{:S(2)}, u32[]{:S(2)}) %collective-permute-start.14) | collective-permute-done | bytes 2097184 | tf_op jit(solution)/shard_map/ppermute | solution.py:90
  132.5 4.7 %fusion.66 = bf16[512,1024]{1,0:T(8,128)(2,1)S(1)} fusion(bf16[4,512,2048]{2,1,0:T(8,128)(2,1)} %bitcast.10, s32[]{:T(128)S(6)} %select_n.222, bf16[1024,1024]{1,0:T(8,128)(2,1)} %collective-permute-done.14, bf16[1024,1024]{1,0:T(8,128)(2,1)S(1)} %copy-done.5), kind=kOutput, calls=%fused_computation.94 | convolution fusion | flops 2156396544 | bytes 7340036 | tf_op jit(solution)/shard_map/dot_general | solution.py:147
  137.2 11.0 %collective-permute-start.15 = (bf16[512,1024]{1,0:T(8,128)(2,1)S(1)}, bf16[512,1024]{1,0:T(8,128)(2,1)S(1)}, u32[]{:S(2)}, u32[]{:S(2)}) collective-permute-start(bf16[512,1024]{1,0:T(8,128)(2,1)S(1)} %fusion.66), channel_id=1, source_target_pairs={{0,8},{4,12},{24,16},{28,20},{1,9},{5,13},{25,17},{29,21},{2,10},{... | collective-permute-start | bytes 3145736 | tf_op jit(solution)/shard_map/ppermute | solution.py:153
  148.3 29.0 %collective-permute-done.8 = bf16[1024,1024]{1,0:T(8,128)(2,1)S(1)} collective-permute-done((bf16[1024,1024]{1,0:T(8,128)(2,1)}, bf16[1024,1024]{1,0:T(8,128)(2,1)S(1)}, u32[]{:S(2)}, u32[]{:S(2)}) %collective-permute-start.8) | collective-permute-done | bytes 2097184 | tf_op jit(solution)/shard_map/ppermute | solution.py:90
  177.3 4.0 fusion.63
  181.3 11.0 %collective-permute-start.9 = (bf16[512,1024]{1,0:T(8,128)(2,1)S(1)}, bf16[512,1024]{1,0:T(8,128)(2,1)S(1)}, u32[]{:S(2)}, u32[]{:S(2)}) collective-permute-start(bf16[512,1024]{1,0:T(8,128)(2,1)S(1)} %fusion.63), channel_id=1, source_target_pairs={{0,8},{4,12},{24,16},{28,20},{1,9},{5,13},{25,17},{29,21},{2,10},{... | collective-permute-start | bytes 3145736 | tf_op jit(solution)/shard_map/ppermute | solution.py:153
  192.5 29.1 %collective-permute-done.20 = bf16[1024,1024]{1,0:T(8,128)(2,1)S(1)} collective-permute-done((bf16[1024,1024]{1,0:T(8,128)(2,1)}, bf16[1024,1024]{1,0:T(8,128)(2,1)S(1)}, u32[]{:S(2)}, u32[]{:S(2)}) %collective-permute-start.20) | collective-permute-done | bytes 2097184 | tf_op jit(solution)/shard_map/ppermute | solution.py:90
  221.6 4.0 fusion.69
  225.5 11.2 %collective-permute-start.21 = (bf16[512,1024]{1,0:T(8,128)(2,1)S(1)}, bf16[512,1024]{1,0:T(8,128)(2,1)S(1)}, u32[]{:S(2)}, u32[]{:S(2)}) collective-permute-start(bf16[512,1024]{1,0:T(8,128)(2,1)S(1)} %fusion.69), channel_id=1, source_target_pairs={{0,8},{4,12},{24,16},{28,20},{1,9},{5,13},{25,17},{29,21},{2,10},{... | collective-permute-start | bytes 3145736 | tf_op jit(solution)/shard_map/ppermute | solution.py:153
  236.8 4.6 %add_convert_fusion.5 = bf16[512,1024]{1,0:T(8,128)(2,1)S(1)} fusion(bf16[512,1024]{1,0:T(8,128)(2,1)S(1)} %collective-permute-done.15, bf16[4,512,2048]{2,1,0:T(8,128)(2,1)} %bitcast.10, s32[]{:T(128)S(6)} %select_n.220, bf16[1024,1024]{1,0:T(8,128)(2,1)} %collective-permute-done.14, bf16[1024,1024]{1,0:T(8,128)(2,1)S(1)} %copy-done.5), kind=kOutput, calls=%fused_computation.74 | convolution fusion | flops 2157445120 | bytes 8388612 | tf_op jit(solution)/shard_map/dot_general | solution.py:147
  242.1 1.9 collective-permute-start.16
  244.0 4.0 add_convert_fusion.8
  248.7 5.7 %collective-permute-start.10 = (bf16[512,1024]{1,0:T(8,128)(2,1)S(1)}, bf16[512,1024]{1,0:T(8,128)(2,1)S(1)}, u32[]{:S(2)}, u32[]{:S(2)}) collective-permute-start(bf16[512,1024]{1,0:T(8,128)(2,1)S(1)} %add_convert_fusion.8), channel_id=1, source_target_pairs={{0,8},{4,12},{8,16},{12,20},{1,9},{5,13},{9,17},{13,21},{2,10},{6,... | collective-permute-start | bytes 3145736 | tf_op jit(solution)/shard_map/ppermute | solution.py:153
  254.4 5.7 %collective-permute-done.21 = bf16[512,1024]{1,0:T(8,128)(2,1)S(1)} collective-permute-done((bf16[512,1024]{1,0:T(8,128)(2,1)S(1)}, bf16[512,1024]{1,0:T(8,128)(2,1)S(1)}, u32[]{:S(2)}, u32[]{:S(2)}) %collective-permute-start.21) | collective-permute-done | bytes 1048608 | tf_op jit(solution)/shard_map/ppermute | solution.py:153
  260.1 4.0 add_convert_fusion.2
  264.8 6.3 %collective-permute-start.22 = (bf16[512,1024]{1,0:T(8,128)(2,1)S(1)}, bf16[512,1024]{1,0:T(8,128)(2,1)S(1)}, u32[]{:S(2)}, u32[]{:S(2)}) collective-permute-start(bf16[512,1024]{1,0:T(8,128)(2,1)S(1)} %add_convert_fusion.2), channel_id=1, source_target_pairs={{0,8},{4,12},{8,16},{12,20},{1,9},{5,13},{9,17},{13,21},{2,10},{6,... | collective-permute-start | bytes 3145736 | tf_op jit(solution)/shard_map/ppermute | solution.py:153
  271.2 4.6 %add_convert_fusion.3 = bf16[512,1024]{1,0:T(8,128)(2,1)S(1)} fusion(bf16[512,1024]{1,0:T(8,128)(2,1)S(1)} %collective-permute-done.17, bf16[4,512,2048]{2,1,0:T(8,128)(2,1)} %bitcast.10, s32[]{:T(128)S(6)} %select_n.230, bf16[1024,1024]{1,0:T(8,128)(2,1)} %collective-permute-done.14, bf16[1024,1024]{1,0:T(8,128)(2,1)S(1)} %copy-done.5), kind=kOutput, calls=%fused_computation.70 | convolution fusion | flops 2157445120 | bytes 8388612 | tf_op jit(solution)/shard_map/dot_general | solution.py:147
  275.8 6.8 %collective-permute-done.16 = bf16[512,1024]{1,0:T(8,128)(2,1)S(1)} collective-permute-done((bf16[512,1024]{1,0:T(8,128)(2,1)S(1)}, bf16[512,1024]{1,0:T(8,128)(2,1)S(1)}, u32[]{:S(2)}, u32[]{:S(2)}) %collective-permute-start.16) | collective-permute-done | bytes 1048608 | tf_op jit(solution)/shard_map/ppermute | solution.py:153
  282.6 4.6 %add_convert_fusion.4 = bf16[512,1024]{1,0:T(8,128)(2,1)S(1)} fusion(bf16[512,1024]{1,0:T(8,128)(2,1)S(1)} %collective-permute-done.16, bf16[4,512,2048]{2,1,0:T(8,128)(2,1)} %bitcast.10, s32[]{:T(128)S(6)} %select_n.227, bf16[1024,1024]{1,0:T(8,128)(2,1)} %collective-permute-done.14, bf16[1024,1024]{1,0:T(8,128)(2,1)S(1)} %copy-done.5), kind=kOutput, calls=%fused_computation.72 | convolution fusion | flops 2157445120 | bytes 8388612 | tf_op jit(solution)/shard_map/dot_general | solution.py:147
  287.2 13.6 %collective-permute-start.18 = (bf16[512,1024]{1,0:T(8,128)(2,1)S(1)}, bf16[512,1024]{1,0:T(8,128)(2,1)S(1)}, u32[]{:S(2)}, u32[]{:S(2)}) collective-permute-start(bf16[512,1024]{1,0:T(8,128)(2,1)S(1)} %add_convert_fusion.4), channel_id=1, source_target_pairs={{0,8},{4,12},{8,16},{12,20},{16,24},{20,28},{1,9},{5,13},{9,17},{1... | collective-permute-start | bytes 3145736 | tf_op jit(solution)/shard_map/ppermute | solution.py:153
  300.8 1.5 collective-permute-start.19
  302.3 4.0 add_convert_fusion.6
  306.3 4.0 add_convert_fusion.7
  310.3 4.6 %collective-permute-start.12 = (bf16[512,1024]{1,0:T(8,128)(2,1)S(1)}, bf16[512,1024]{1,0:T(8,128)(2,1)S(1)}, u32[]{:S(2)}, u32[]{:S(2)}) collective-permute-start(bf16[512,1024]{1,0:T(8,128)(2,1)S(1)} %add_convert_fusion.7), channel_id=1, source_target_pairs={{0,8},{4,12},{8,16},{12,20},{16,24},{20,28},{1,9},{5,13},{9,17},{1... | collective-permute-start | bytes 3145736 | tf_op jit(solution)/shard_map/ppermute | solution.py:153
  314.9 1.3 collective-permute-start.13
  316.2 4.0 add_convert_fusion
  320.2 7.3 %collective-permute-done.22 = bf16[512,1024]{1,0:T(8,128)(2,1)S(1)} collective-permute-done((bf16[512,1024]{1,0:T(8,128)(2,1)S(1)}, bf16[512,1024]{1,0:T(8,128)(2,1)S(1)}, u32[]{:S(2)}, u32[]{:S(2)}) %collective-permute-start.22) | collective-permute-done | bytes 1048608 | tf_op jit(solution)/shard_map/ppermute | solution.py:153
  327.5 4.0 add_convert_fusion.1
  331.5 4.7 %collective-permute-start.24 = (bf16[512,1024]{1,0:T(8,128)(2,1)S(1)}, bf16[512,1024]{1,0:T(8,128)(2,1)S(1)}, u32[]{:S(2)}, u32[]{:S(2)}) collective-permute-start(bf16[512,1024]{1,0:T(8,128)(2,1)S(1)} %add_convert_fusion.1), channel_id=1, source_target_pairs={{0,8},{4,12},{8,16},{12,20},{16,24},{20,28},{1,9},{5,13},{9,17},{1... | collective-permute-start | bytes 3145736 | tf_op jit(solution)/shard_map/ppermute | solution.py:153
  336.2 4.6 %fusion.24 = f32[512,1024]{1,0:T(8,128)S(1)} fusion(bf16[4,512,2048]{2,1,0:T(8,128)(2,1)} %bitcast.10, s32[]{:T(128)S(6)} %select_n.231, bf16[1024,1024]{1,0:T(8,128)(2,1)} %collective-permute-done.14, bf16[1024,1024]{1,0:T(8,128)(2,1)S(1)} %copy-done.5), kind=kOutput, calls=%fused_computation.36 | convolution fusion | flops 2155872256 | bytes 8388612 | tf_op jit(solution)/shard_map/dot_general | solution.py:147
  340.8 4.0 fusion.30
  344.8 4.0 fusion.18
  351.8 20.7 %collective-permute-done.12 = bf16[512,1024]{1,0:T(8,128)(2,1)S(1)} collective-permute-done((bf16[512,1024]{1,0:T(8,128)(2,1)S(1)}, bf16[512,1024]{1,0:T(8,128)(2,1)S(1)}, u32[]{:S(2)}, u32[]{:S(2)}) %collective-permute-start.12) | collective-permute-done | bytes 1048608 | tf_op jit(solution)/shard_map/ppermute | solution.py:153
  373.0 20.3 %collective-permute-done.24 = bf16[512,1024]{1,0:T(8,128)(2,1)S(1)} collective-permute-done((bf16[512,1024]{1,0:T(8,128)(2,1)S(1)}, bf16[512,1024]{1,0:T(8,128)(2,1)S(1)}, u32[]{:S(2)}, u32[]{:S(2)}) %collective-permute-start.24) | collective-permute-done | bytes 1048608 | tf_op jit(solution)/shard_map/ppermute | solution.py:153
  393.9 1.3 copy-done.4
  395.2 4.4 collective-permute-start.26
  399.7 1.4 collective-permute-done.26
  401.0 6.0 %fusion.10 = f32[64,8,8,128]{3,1,2,0:T(8,128)S(1)} fusion(f32[2,1024]{1,0:T(2,128)S(1)} %get-tuple-element.74, f32[512,1024]{1,0:T(8,128)} %copy-done.4, f32[2,1024]{1,0:T(2,128)S(1)} %get-tuple-element.75, f32[512,1024]{1,0:T(8,128)} %copy-done.3, f32[1024]{0:T(1024)S(1)} %bitcast.167, f32[1024]{0:T(1024)S(1)} %bitcast.168, f32[1024]{0:T(1024)S(1)} %bitcast.169, ...), kind=kLoop, calls=%fused_computation.19 | loop fusion | flops 7864320 | bytes 6332416
  407.5 2.4 shard_map.64
  409.9 4.9 %collective-permute-start.27 = (f32[16,8,128]{2,1,0:T(8,128)S(1)}, f32[16,8,128]{2,1,0:T(8,128)S(1)}, u32[]{:S(2)}, u32[]{:S(2)}) collective-permute-start(f32[16,8,128]{2,1,0:T(8,128)S(1)} %shard_map.64), channel_id=1, source_target_pairs={{0,8},{4,12},{8,16},{12,20},{16,24},{20,28},{1,9},{5,13},{9,17},{1... | collective-permute-start | bytes 196616 | tf_op jit(solution)/shard_map/ppermute | solution.py:84
  414.8 3.7 collective-permute-start.28
  418.5 1.3 collective-permute-start.29
  421.7 5.2 %shard_map.65 = f32[512,8,128]{2,1,0:T(8,128)S(1)} custom-call(f32[512,8,128]{2,1,0:T(8,128)S(1)} %bitcast.159, f32[512,8,128]{2,1,0:T(8,128)S(1)} %bitcast.160, f32[16,8,128]{2,1,0:T(8,128)S(1)} %bitcast.162, f32[16,8,128]{2,1,0:T(8,128)S(1)} %bitcast.163, f32[8,128]{1,0:T(8,128)S(1)} %dynamic-slice_bitcast_fusion.8.skip_ref, ...), custom_call_target="tpu_custom_call" | custom-call | tf_op jit(solution)/shard_map/pallas_call | solution.py:203
  427.5 1.6 collective-permute-start.30
  429.3 8.9 %collective-permute-done.30 = bf16[256,1024]{1,0:T(8,128)(2,1)S(1)} collective-permute-done((bf16[256,1024]{1,0:T(8,128)(2,1)S(1)}, bf16[256,1024]{1,0:T(8,128)(2,1)S(1)}, u32[]{:S(2)}, u32[]{:S(2)}) %collective-permute-start.30) | collective-permute-done | bytes 524320 | tf_op jit(solution)/shard_map/ppermute | solution.py:90
  (79 shorter events, 12.5 us)
Async XLA Ops:
  0.0 399.5 %copy-start = (f32[2048]{0:T(1024)S(1)}, f32[2048]{0:T(1024)}, u32[]{:S(2)}) copy-start(f32[2048]{0:T(1024)} %param.11) | copy-start | bytes 24580
  0.0 12.3 %collective-permute-start = (bf16[256,2048]{1,0:T(8,128)(2,1)}, bf16[256,2048]{1,0:T(8,128)(2,1)S(1)}, u32[]{:S(2)}, u32[]{:S(2)}) collective-permute-start(bf16[256,2048]{1,0:T(8,128)(2,1)} %param.6), channel_id=1, source_target_pairs={{0,0},{1,8},{2,16},{3,24},{4,4},{5,12},{6,20},{7,28},{8,1},{9,9},{... | collective-permute-start | bytes 3145736 | tf_op jit(solution)/shard_map/ppermute | solution.py:107
  18.2 55.8 %collective-permute-start.2 = (bf16[256,2048]{1,0:T(8,128)(2,1)S(1)}, bf16[256,2048]{1,0:T(8,128)(2,1)}, u32[]{:S(2)}, u32[]{:S(2)}) collective-permute-start(bf16[256,2048]{1,0:T(8,128)(2,1)S(1)} %get-tuple-element.46), channel_id=1, source_target_pairs={{0,2},{1,3},{2,0},{3,1},{4,6},{5,7},{6,4},{7,5},{8,10},{9,11},{10,... | collective-permute-start | bytes 3145736 | tf_op jit(solution)/shard_map/ppermute | solution.py:119
  61.1 14.8 %collective-permute-start.4 = (bf16[256,2048]{1,0:T(8,128)(2,1)S(1)}, bf16[256,2048]{1,0:T(8,128)(2,1)S(1)}, u32[]{:S(2)}, u32[]{:S(2)}) collective-permute-start(bf16[256,2048]{1,0:T(8,128)(2,1)S(1)} %collective-permute-done), channel_id=1, source_target_pairs={{0,4},{4,0},{8,12},{12,8},{16,20},{20,16},{24,28},{28,24},{1,5},{5... | collective-permute-start | bytes 3145736 | tf_op jit(solution)/shard_map/ppermute | solution.py:90
  62.6 13.4 %collective-permute-start.1 = (bf16[256,2048]{1,0:T(8,128)(2,1)S(1)}, bf16[256,2048]{1,0:T(8,128)(2,1)}, u32[]{:S(2)}, u32[]{:S(2)}) collective-permute-start(bf16[256,2048]{1,0:T(8,128)(2,1)S(1)} %get-tuple-element.46), channel_id=1, source_target_pairs={{0,1},{1,0},{2,3},{3,2},{4,5},{5,4},{6,7},{7,6},{8,9},{9,8},{10,11... | collective-permute-start | bytes 3145736 | tf_op jit(solution)/shard_map/ppermute | solution.py:122
  74.0 6.8 %collective-permute-start.3 = (bf16[256,2048]{1,0:T(8,128)(2,1)}, bf16[256,2048]{1,0:T(8,128)(2,1)S(1)}, u32[]{:S(2)}, u32[]{:S(2)}) collective-permute-start(bf16[256,2048]{1,0:T(8,128)(2,1)} %collective-permute-done.2), channel_id=1, source_target_pairs={{0,1},{1,0},{2,3},{3,2},{4,5},{5,4},{6,7},{7,6},{8,9},{9,8},{10,11... | collective-permute-start | bytes 3145736 | tf_op jit(solution)/shard_map/ppermute | solution.py:122
  78.3 6.8 %copy-start.2 = (bf16[1024,1,2048]{2,0,1:T(8,128)(2,1)S(1)}, bf16[1024,1,2048]{2,0,1:T(8,128)(2,1)}, u32[]{:S(2)}) copy-start(bf16[1024,1,2048]{2,0,1:T(8,128)(2,1)} %get-tuple-element.49) | copy-start | bytes 12582916
  81.8 3.3 copy-start.1
  83.3 24.1 %collective-permute-start.6 = (bf16[256,2048]{1,0:T(8,128)(2,1)S(1)}, bf16[256,2048]{1,0:T(8,128)(2,1)}, u32[]{:S(2)}, u32[]{:S(2)}) collective-permute-start(bf16[256,2048]{1,0:T(8,128)(2,1)S(1)} %get-tuple-element.44), channel_id=1, source_target_pairs={{0,2},{1,3},{2,0},{3,1},{4,6},{5,7},{6,4},{7,5},{8,10},{9,11},{10,... | collective-permute-start | bytes 3145736 | tf_op jit(solution)/shard_map/ppermute | solution.py:119
  83.4 26.2 %collective-permute-start.5 = (bf16[256,2048]{1,0:T(8,128)(2,1)S(1)}, bf16[256,2048]{1,0:T(8,128)(2,1)}, u32[]{:S(2)}, u32[]{:S(2)}) collective-permute-start(bf16[256,2048]{1,0:T(8,128)(2,1)S(1)} %get-tuple-element.44), channel_id=1, source_target_pairs={{0,1},{1,0},{2,3},{3,2},{4,5},{5,4},{6,7},{7,6},{8,9},{9,8},{10,11... | collective-permute-start | bytes 3145736 | tf_op jit(solution)/shard_map/ppermute | solution.py:122
  83.7 48.8 %collective-permute-start.14 = (bf16[1024,1024]{1,0:T(8,128)(2,1)}, bf16[1024,1024]{1,0:T(8,128)(2,1)}, u32[]{:S(2)}, u32[]{:S(2)}) collective-permute-start(bf16[1024,1024]{1,0:T(8,128)(2,1)} %get-tuple-element.31), channel_id=1, source_target_pairs={{0,4},{4,0},{8,12},{12,8},{16,20},{20,16},{24,28},{28,24},{1,5},{5... | collective-permute-start | bytes 6291464 | tf_op jit(solution)/shard_map/ppermute | solution.py:90
  85.1 22.3 %copy-start.10 = (bf16[3,3,2048]{2,1,0:T(4,128)(2,1)S(1)}, bf16[3,3,2048]{2,1,0:T(4,128)(2,1)}, u32[]{:S(2)}) copy-start(bf16[3,3,2048]{2,1,0:T(4,128)(2,1)} %param.8) | copy-start | bytes 110596
  107.4 7.0 %collective-permute-start.7 = (bf16[256,2048]{1,0:T(8,128)(2,1)}, bf16[256,2048]{1,0:T(8,128)(2,1)}, u32[]{:S(2)}, u32[]{:S(2)}) collective-permute-start(bf16[256,2048]{1,0:T(8,128)(2,1)} %collective-permute-done.6), channel_id=1, source_target_pairs={{0,1},{1,0},{2,3},{3,2},{4,5},{5,4},{6,7},{7,6},{8,9},{9,8},{10,11... | collective-permute-start | bytes 3145736 | tf_op jit(solution)/shard_map/ppermute | solution.py:122
  107.5 69.8 %collective-permute-start.8 = (bf16[1024,1024]{1,0:T(8,128)(2,1)}, bf16[1024,1024]{1,0:T(8,128)(2,1)S(1)}, u32[]{:S(2)}, u32[]{:S(2)}) collective-permute-start(bf16[1024,1024]{1,0:T(8,128)(2,1)} %get-tuple-element.25), channel_id=1, source_target_pairs={{0,4},{4,0},{8,12},{12,8},{16,20},{20,16},{24,28},{28,24},{1,5},{5... | collective-permute-start | bytes 6291464 | tf_op jit(solution)/shard_map/ppermute | solution.py:90
  109.0 112.6 %collective-permute-start.20 = (bf16[1024,1024]{1,0:T(8,128)(2,1)}, bf16[1024,1024]{1,0:T(8,128)(2,1)S(1)}, u32[]{:S(2)}, u32[]{:S(2)}) collective-permute-start(bf16[1024,1024]{1,0:T(8,128)(2,1)} %get-tuple-element.37), channel_id=1, source_target_pairs={{0,4},{4,0},{8,12},{12,8},{16,20},{20,16},{24,28},{28,24},{1,5},{5... | collective-permute-start | bytes 6291464 | tf_op jit(solution)/shard_map/ppermute | solution.py:90
  111.9 20.6 %copy-start.5 = (bf16[1024,1024]{1,0:T(8,128)(2,1)S(1)}, bf16[1024,1024]{1,0:T(8,128)(2,1)}, u32[]{:S(2)}) copy-start(bf16[1024,1024]{1,0:T(8,128)(2,1)} %get-tuple-element.50) | copy-start | bytes 6291460
  132.5 44.8 %copy-start.6 = (bf16[1024,1024]{1,0:T(8,128)(2,1)S(1)}, bf16[1024,1024]{1,0:T(8,128)(2,1)}, u32[]{:S(2)}) copy-start(bf16[1024,1024]{1,0:T(8,128)(2,1)} %get-tuple-element.77) | copy-start | bytes 6291460
  137.2 99.5 %collective-permute-start.15 = (bf16[512,1024]{1,0:T(8,128)(2,1)S(1)}, bf16[512,1024]{1,0:T(8,128)(2,1)S(1)}, u32[]{:S(2)}, u32[]{:S(2)}) collective-permute-start(bf16[512,1024]{1,0:T(8,128)(2,1)S(1)} %fusion.66), channel_id=1, source_target_pairs={{0,8},{4,12},{24,16},{28,20},{1,9},{5,13},{25,17},{29,21},{2,10},{... | collective-permute-start | bytes 3145736 | tf_op jit(solution)/shard_map/ppermute | solution.py:153
  177.3 15.1 %copy-start.8 = (f32[2048,16]{0,1:T(8,128)S(1)}, f32[2048,16]{0,1:T(8,128)}, u32[]{:S(2)}) copy-start(f32[2048,16]{0,1:T(8,128)} %param.9) | copy-start | bytes 393220
  177.3 15.1 %copy-start.9 = (f32[2048,16]{0,1:T(8,128)S(1)}, f32[2048,16]{0,1:T(8,128)}, u32[]{:S(2)}) copy-start(f32[2048,16]{0,1:T(8,128)} %param.10) | copy-start | bytes 393220
  181.3 62.6 %collective-permute-start.9 = (bf16[512,1024]{1,0:T(8,128)(2,1)S(1)}, bf16[512,1024]{1,0:T(8,128)(2,1)S(1)}, u32[]{:S(2)}, u32[]{:S(2)}) collective-permute-start(bf16[512,1024]{1,0:T(8,128)(2,1)S(1)} %fusion.63), channel_id=1, source_target_pairs={{0,8},{4,12},{24,16},{28,20},{1,9},{5,13},{25,17},{29,21},{2,10},{... | collective-permute-start | bytes 3145736 | tf_op jit(solution)/shard_map/ppermute | solution.py:153
  225.5 34.6 %collective-permute-start.21 = (bf16[512,1024]{1,0:T(8,128)(2,1)S(1)}, bf16[512,1024]{1,0:T(8,128)(2,1)S(1)}, u32[]{:S(2)}, u32[]{:S(2)}) collective-permute-start(bf16[512,1024]{1,0:T(8,128)(2,1)S(1)} %fusion.69), channel_id=1, source_target_pairs={{0,8},{4,12},{24,16},{28,20},{1,9},{5,13},{25,17},{29,21},{2,10},{... | collective-permute-start | bytes 3145736 | tf_op jit(solution)/shard_map/ppermute | solution.py:153
  241.4 23.5 %collective-permute-start.17 = (bf16[512,1024]{1,0:T(8,128)(2,1)S(1)}, bf16[512,1024]{1,0:T(8,128)(2,1)S(1)}, u32[]{:S(2)}, u32[]{:S(2)}) collective-permute-start(bf16[512,1024]{1,0:T(8,128)(2,1)S(1)} %add_convert_fusion.5), channel_id=1, source_target_pairs={{24,16},{28,20},{16,8},{20,12},{25,17},{29,21},{17,9},{21,13},{26,... | collective-permute-start | bytes 3145736 | tf_op jit(solution)/shard_map/ppermute | solution.py:153
  242.1 40.5 %collective-permute-start.16 = (bf16[512,1024]{1,0:T(8,128)(2,1)S(1)}, bf16[512,1024]{1,0:T(8,128)(2,1)S(1)}, u32[]{:S(2)}, u32[]{:S(2)}) collective-permute-start(bf16[512,1024]{1,0:T(8,128)(2,1)S(1)} %add_convert_fusion.5), channel_id=1, source_target_pairs={{0,8},{4,12},{8,16},{12,20},{1,9},{5,13},{9,17},{13,21},{2,10},{6,... | collective-permute-start | bytes 3145736 | tf_op jit(solution)/shard_map/ppermute | solution.py:153
  248.0 52.8 %collective-permute-start.11 = (bf16[512,1024]{1,0:T(8,128)(2,1)S(1)}, bf16[512,1024]{1,0:T(8,128)(2,1)S(1)}, u32[]{:S(2)}, u32[]{:S(2)}) collective-permute-start(bf16[512,1024]{1,0:T(8,128)(2,1)S(1)} %add_convert_fusion.8), channel_id=1, source_target_pairs={{24,16},{28,20},{16,8},{20,12},{25,17},{29,21},{17,9},{21,13},{26,... | collective-permute-start | bytes 3145736 | tf_op jit(solution)/shard_map/ppermute | solution.py:153
  248.7 57.6 %collective-permute-start.10 = (bf16[512,1024]{1,0:T(8,128)(2,1)S(1)}, bf16[512,1024]{1,0:T(8,128)(2,1)S(1)}, u32[]{:S(2)}, u32[]{:S(2)}) collective-permute-start(bf16[512,1024]{1,0:T(8,128)(2,1)S(1)} %add_convert_fusion.8), channel_id=1, source_target_pairs={{0,8},{4,12},{8,16},{12,20},{1,9},{5,13},{9,17},{13,21},{2,10},{6,... | collective-permute-start | bytes 3145736 | tf_op jit(solution)/shard_map/ppermute | solution.py:153
  264.1 50.8 %collective-permute-start.23 = (bf16[512,1024]{1,0:T(8,128)(2,1)S(1)}, bf16[512,1024]{1,0:T(8,128)(2,1)S(1)}, u32[]{:S(2)}, u32[]{:S(2)}) collective-permute-start(bf16[512,1024]{1,0:T(8,128)(2,1)S(1)} %add_convert_fusion.2), channel_id=1, source_target_pairs={{24,16},{28,20},{16,8},{20,12},{25,17},{29,21},{17,9},{21,13},{26,... | collective-permute-start | bytes 3145736 | tf_op jit(solution)/shard_map/ppermute | solution.py:153
  264.8 62.7 %collective-permute-start.22 = (bf16[512,1024]{1,0:T(8,128)(2,1)S(1)}, bf16[512,1024]{1,0:T(8,128)(2,1)S(1)}, u32[]{:S(2)}, u32[]{:S(2)}) collective-permute-start(bf16[512,1024]{1,0:T(8,128)(2,1)S(1)} %add_convert_fusion.2), channel_id=1, source_target_pairs={{0,8},{4,12},{8,16},{12,20},{1,9},{5,13},{9,17},{13,21},{2,10},{6,... | collective-permute-start | bytes 3145736 | tf_op jit(solution)/shard_map/ppermute | solution.py:153
  287.2 62.8 %collective-permute-start.18 = (bf16[512,1024]{1,0:T(8,128)(2,1)S(1)}, bf16[512,1024]{1,0:T(8,128)(2,1)S(1)}, u32[]{:S(2)}, u32[]{:S(2)}) collective-permute-start(bf16[512,1024]{1,0:T(8,128)(2,1)S(1)} %add_convert_fusion.4), channel_id=1, source_target_pairs={{0,8},{4,12},{8,16},{12,20},{16,24},{20,28},{1,9},{5,13},{9,17},{1... | collective-permute-start | bytes 3145736 | tf_op jit(solution)/shard_map/ppermute | solution.py:153
  300.8 50.5 %collective-permute-start.19 = (bf16[512,1024]{1,0:T(8,128)(2,1)S(1)}, bf16[512,1024]{1,0:T(8,128)(2,1)S(1)}, u32[]{:S(2)}, u32[]{:S(2)}) collective-permute-start(bf16[512,1024]{1,0:T(8,128)(2,1)S(1)} %add_convert_fusion.3), channel_id=1, source_target_pairs={{24,16},{28,20},{16,8},{20,12},{8,0},{12,4},{25,17},{29,21},{17,9}... | collective-permute-start | bytes 3145736 | tf_op jit(solution)/shard_map/ppermute | solution.py:153
  310.3 62.2 %collective-permute-start.12 = (bf16[512,1024]{1,0:T(8,128)(2,1)S(1)}, bf16[512,1024]{1,0:T(8,128)(2,1)S(1)}, u32[]{:S(2)}, u32[]{:S(2)}) collective-permute-start(bf16[512,1024]{1,0:T(8,128)(2,1)S(1)} %add_convert_fusion.7), channel_id=1, source_target_pairs={{0,8},{4,12},{8,16},{12,20},{16,24},{20,28},{1,9},{5,13},{9,17},{1... | collective-permute-start | bytes 3145736 | tf_op jit(solution)/shard_map/ppermute | solution.py:153
  314.9 57.6 %collective-permute-start.13 = (bf16[512,1024]{1,0:T(8,128)(2,1)S(1)}, bf16[512,1024]{1,0:T(8,128)(2,1)S(1)}, u32[]{:S(2)}, u32[]{:S(2)}) collective-permute-start(bf16[512,1024]{1,0:T(8,128)(2,1)S(1)} %add_convert_fusion.6), channel_id=1, source_target_pairs={{24,16},{28,20},{16,8},{20,12},{8,0},{12,4},{25,17},{29,21},{17,9}... | collective-permute-start | bytes 3145736 | tf_op jit(solution)/shard_map/ppermute | solution.py:153
  331.5 61.8 %collective-permute-start.24 = (bf16[512,1024]{1,0:T(8,128)(2,1)S(1)}, bf16[512,1024]{1,0:T(8,128)(2,1)S(1)}, u32[]{:S(2)}, u32[]{:S(2)}) collective-permute-start(bf16[512,1024]{1,0:T(8,128)(2,1)S(1)} %add_convert_fusion.1), channel_id=1, source_target_pairs={{0,8},{4,12},{8,16},{12,20},{16,24},{20,28},{1,9},{5,13},{9,17},{1... | collective-permute-start | bytes 3145736 | tf_op jit(solution)/shard_map/ppermute | solution.py:153
  350.0 43.3 %collective-permute-start.25 = (bf16[512,1024]{1,0:T(8,128)(2,1)S(1)}, bf16[512,1024]{1,0:T(8,128)(2,1)S(1)}, u32[]{:S(2)}, u32[]{:S(2)}) collective-permute-start(bf16[512,1024]{1,0:T(8,128)(2,1)S(1)} %add_convert_fusion), channel_id=1, source_target_pairs={{24,16},{28,20},{16,8},{20,12},{8,0},{12,4},{25,17},{29,21},{17,9}... | collective-permute-start | bytes 3145736 | tf_op jit(solution)/shard_map/ppermute | solution.py:153
  373.0 20.8 %copy-start.3 = (f32[512,1024]{1,0:T(8,128)}, f32[512,1024]{1,0:T(8,128)S(1)}, u32[]{:S(2)}) copy-start(f32[512,1024]{1,0:T(8,128)S(1)} %convert_add_fusion.2) | copy-start | bytes 6291460
  393.8 1.3 copy-start.4
  395.2 5.9 %collective-permute-start.26 = (f32[3,2,1024]{2,1,0:T(2,128)S(1)}, f32[3,2,1024]{2,1,0:T(2,128)S(1)}, u32[]{:S(2)}, u32[]{:S(2)}) collective-permute-start(f32[3,2,1024]{2,1,0:T(2,128)S(1)} %pad_maximum_fusion.6), channel_id=1, source_target_pairs={{0,8},{4,12},{8,16},{12,20},{16,24},{20,28},{1,9},{5,13},{9,17},{1... | collective-permute-start | bytes 73736 | tf_op jit(solution)/shard_map/ppermute | solution.py:84
  409.9 10.9 %collective-permute-start.27 = (f32[16,8,128]{2,1,0:T(8,128)S(1)}, f32[16,8,128]{2,1,0:T(8,128)S(1)}, u32[]{:S(2)}, u32[]{:S(2)}) collective-permute-start(f32[16,8,128]{2,1,0:T(8,128)S(1)} %shard_map.64), channel_id=1, source_target_pairs={{0,8},{4,12},{8,16},{12,20},{16,24},{20,28},{1,9},{5,13},{9,17},{1... | collective-permute-start | bytes 196616 | tf_op jit(solution)/shard_map/ppermute | solution.py:84
  414.8 6.1 %collective-permute-start.28 = (f32[16,8,128]{2,1,0:T(8,128)S(1)}, f32[16,8,128]{2,1,0:T(8,128)S(1)}, u32[]{:S(2)}, u32[]{:S(2)}) collective-permute-start(f32[16,8,128]{2,1,0:T(8,128)S(1)} %shard_map.64), channel_id=1, source_target_pairs={{0,16},{4,20},{8,24},{12,28},{1,17},{5,21},{9,25},{13,29},{2,18},{... | collective-permute-start | bytes 196616 | tf_op jit(solution)/shard_map/ppermute | solution.py:84
  418.5 3.2 collective-permute-start.29
  427.5 10.7 %collective-permute-start.30 = (bf16[256,1024]{1,0:T(8,128)(2,1)S(1)}, bf16[256,1024]{1,0:T(8,128)(2,1)S(1)}, u32[]{:S(2)}, u32[]{:S(2)}) collective-permute-start(bf16[256,1024]{1,0:T(8,128)(2,1)S(1)} %dynamic-slice_bitcast_fusion.6), channel_id=1, source_target_pairs={{0,4},{4,0},{8,12},{12,8},{16,20},{20,16},{24,28},{28,24},{1,5},{5... | collective-permute-start | bytes 1572872 | tf_op jit(solution)/shard_map/ppermute | solution.py:90
  429.3 8.9 %copy-start.7 = (bf16[256,2048]{1,0:T(8,128)(2,1)}, bf16[256,2048]{1,0:T(8,128)(2,1)S(1)}, u32[]{:S(2)}) copy-start(bf16[256,2048]{1,0:T(8,128)(2,1)S(1)} %bitcast_dynamic-update-slice_fusion.8) | copy-start | bytes 3145732
where the time goes:
time: 448 us; the launch traced here: 439 us
  waiting for transfers between devices  180 us (40%)
  starting transfers between devices  142 us (32%)
  matrix products  62.9 us (14%)
  local copies, waits for them, and re-layouts  34.5 us (8%)
  other arithmetic  11.2 us (2%)
  Pallas kernels  7.56 us (2%)
    ppermute x5, waiting for transfers between devices, along_x(): return lax.ppermute(block, 'ctx', route)  84.7 us
    ppermute x15, starting transfers between devices, hops(): lax.ppermute(block, 'ctx', [(i * n_x + k, j * n_x + k) for i, j in pairs...  76.4 us
    dot_general x15, matrix products, share(): return jnp.dot(block, weights[g], preferred_element_type=jnp.float32)  62.9 us
    ppermute x15, waiting for transfers between devices, hops(): lax.ppermute(block, 'ctx', [(i * n_x + k, j * n_x + k) for i, j in pairs...  62 us
    ppermute x2, starting transfers between devices, along_outer(): return lax.ppermute(block, 'ch', route)  43 us
    ppermute x2, waiting for transfers between devices, along_outer(): return lax.ppermute(block, 'ch', route)  30.9 us
    ppermute x4, starting transfers between devices, along_z(): return lax.ppermute(block, 'ctx', route)  14.2 us
    dynamic_update_slice x6, local copies, waits for them, and re-layouts, local(): lax.dynamic_update_slice(found, piece[None, None], (owner, (x - hop) % n_...  13 us
  transfers between devices with their start and end apart: 31, of which 15 were waited for; matrix products, arithmetic and copies ran while one was open for 21% of the time, Pallas kernels for 0%

commit v1 on v0

--- a/solution.py
+++ b/solution.py
@@ -111,6 +111,9 @@
     if n_q == 1:
         beside = [rolled(block, x, feats, n_x) for block in beside]
 
+    came[0], beside[1:], away[1] = lax.optimization_barrier((came[0], beside[1:], away[1]))
+    came.append(exchange(1))
+
     mine = lax.axis_index("ch")
     outer = n_ch // CORES
 
@@ -131,20 +134,19 @@
                 found = lax.dynamic_update_slice(
                     found, piece[None, None], (owner, (x - hop) % n_x, 0, 0)
                 )
-    beside, away[1:] = lax.optimization_barrier((beside, away[1:]))
-    came += [exchange(g) for g in range(1, streams)]
+    found, came[1], away[2] = lax.optimization_barrier((found, came[1], away[2]))
+    came.append(exchange(2))
     found = found.reshape(LINE, n_q, n_x, tok_rows, tokens.shape[1])
     plane = found.transpose(0, 2, 3, 1, 4).reshape(LINE, rows, n_x * feats)
     if n_q > 1:
         plane = rolled(plane, x, feats, n_x)
 
-    weights = [
-        jnp.concatenate([weight_part(g, x)] + came[g][::-1], axis=0) for g in range(streams)
-    ]
-
-    def share(g, index, source):
+    def gathered_weight(g):
+        return jnp.concatenate([weight_part(g, x)] + came[g][::-1], axis=0)
+
+    def share(weight, index, source):
         block = lax.dynamic_index_in_dim(source, index, 0, keepdims=False)
-        return jnp.dot(block, weights[g], preferred_element_type=jnp.float32)
+        return jnp.dot(block, weight, preferred_element_type=jnp.float32)
 
     def choose(values):
         return sum(jnp.where(z == i, value, 0) for i, value in enumerate(values))
@@ -161,15 +163,18 @@
     low, wide = jnp.bfloat16, jnp.float32
 
     def reduce_stream(g):
-        one = hops(share(g, first, plane).astype(low), [(0, 1), (3, 2)])
-        two = (share(g, second, plane) + one.astype(wide)).astype(low)
+        weight = gathered_weight(g)
+        one = hops(share(weight, first, plane).astype(low), [(0, 1), (3, 2)])
+        two = (share(weight, second, plane) + one.astype(wide)).astype(low)
+        if g == 0:
+            two, came[2] = lax.optimization_barrier((two, came[2]))
         two, later = lax.optimization_barrier((two, plane))
         up, down = hops(two, [(0, 1), (1, 2)]), hops(two, [(3, 2), (2, 1)])
-        up = (share(g, third_up, later) + up.astype(wide)).astype(low)
-        down = (share(g, third_down, later) + down.astype(wide)).astype(low)
+        up = (share(weight, third_up, later) + up.astype(wide)).astype(low)
+        down = (share(weight, third_down, later) + down.astype(wide)).astype(low)
         up, down, later = lax.optimization_barrier((up, down, later))
         up, down = hops(up, [(0, 1), (1, 2), (2, 3)]), hops(down, [(3, 2), (2, 1), (1, 0)])
-        return share(g, z, later) + up.astype(wide) + down.astype(wide)
+        return share(weight, z, later) + up.astype(wide) + down.astype(wide)
 
     taps = lax.dynamic_slice_in_dim(short_filter, x * part, part, axis=2).astype(jnp.float32)
     tap_count = taps.shape[0]

time: 448 us -> 440 us (0.982)
  waiting for transfers between devices: 180 us -> 159 us
  matrix products: 62.9 us -> 70.4 us
  starting transfers between devices: 142 us -> 148 us
    ppermute x5, waiting for transfers between devices: 84.7 us -> 53 us  [along_x(): return lax.ppermute(block, 'ctx', route)]
    ppermute x15, waiting for transfers between devices: 62 us -> 93.2 us  [hops(): lax.ppermute(block, 'ctx', [(i * n_x + k, j * n_x + k) for i, j in pairs...]
    ppermute x2, waiting for transfers between devices: 30.9 us -> 10.6 us  [along_outer(): return lax.ppermute(block, 'ch', route)]
    ppermute x2, starting transfers between devices: 43 us -> 61.4 us  [along_outer(): return lax.ppermute(block, 'ch', route)]
    ppermute x15, starting transfers between devices: 76.4 us -> 64.3 us  [hops(): lax.ppermute(block, 'ctx', [(i * n_x + k, j * n_x + k) for i, j in pairs...]
    dot_general x15, matrix products: 62.9 us -> 70.4 us  [share(): return jnp.dot(block, weight, preferred_element_type=jnp.float32)]
    dynamic_slice x2 -> x3, local copies, waits for them, and re-layouts: 5.32 us -> 9.79 us  [weight_part(): return lax.dynamic_slice_in_dim(in_weight[:, g], index * part, part, axis=1)]
    dynamic_update_slice x6 -> x7, local copies, waits for them, and re-layouts: 13 us -> 10.1 us  [local(): lax.dynamic_update_slice(found, piece[None, None], (owner, (x - hop) % n_...]
  transfers between devices with their start and end apart: 31 -> 31, of which waited for: 15 -> 15; matrix products, arithmetic and copies ran while one was open for 21% -> 23% of each run, Pallas kernels for 0% -> 0%
where the time goes in v1:
time: 440 us; the launch traced here: 432 us
  waiting for transfers between devices  159 us (36%)
  starting transfers between devices  148 us (34%)
  matrix products  70.4 us (16%)
  local copies, waits for them, and re-layouts  35.3 us (8%)
  other arithmetic  10.7 us (2%)
  Pallas kernels  7.56 us (2%)
    ppermute x15, waiting for transfers between devices, hops(): lax.ppermute(block, 'ctx', [(i * n_x + k, j * n_x + k) for i, j in pairs...  93.2 us
    dot_general x15, matrix products, share(): return jnp.dot(block, weight, preferred_element_type=jnp.float32)  70.4 us
    ppermute x15, starting transfers between devices, hops(): lax.ppermute(block, 'ctx', [(i * n_x + k, j * n_x + k) for i, j in pairs...  64.3 us
    ppermute x2, starting transfers between devices, along_outer(): return lax.ppermute(block, 'ch', route)  61.4 us
    ppermute x5, waiting for transfers between devices, along_x(): return lax.ppermute(block, 'ctx', route)  53 us
    ppermute x4, starting transfers between devices, along_z(): return lax.ppermute(block, 'ctx', route)  11.6 us
    ppermute x2, waiting for transfers between devices, along_outer(): return lax.ppermute(block, 'ch', route)  10.6 us
    dynamic_update_slice x7, local copies, waits for them, and re-layouts, local(): lax.dynamic_update_slice(found, piece[None, None], (owner, (x - hop) % n_...  10.1 us
  transfers between devices with their start and end apart: 31, of which 15 were waited for; matrix products, arithmetic and copies ran while one was open for 23% of the time, Pallas kernels for 0%

profile of v1, /device:TPU:0, one launch (start us, length us, event | category | flops | bytes accessed | tf_op | source)
XLA Modules:
  0.0 431.7 jit_solution(2971871323959682991)
XLA Ops:
  0.0 2.0 collective-permute-start
  2.0 7.0 %fusion.107 = (bf16[1024,1,2048]{2,0,1:T(8,128)(2,1)}, bf16[1024,1,2048]{2,0,1:T(8,128)(2,1)S(1)}, bf16[1024,1,2048]{2,0,1:T(8,128)(2,1)S(1)}) fusion(bf16[1024,3,2048]{2,0,1:T(8,128)(2,1)} %param.7), kind=kLoop, calls=%fused_computation.144 | loop fusion | bytes 25165824 | tf_op jit(solution)/shard_map/slice | solution.py:93
  9.0 2.6 dynamic-slice_bitcast_fusion.1
  11.7 3.0 collective-permute-start.4
  14.7 4.4 %broadcast_in_dim.31 = bf16[4,2,256,2048]{3,2,1,0:T(8,128)(2,1)} broadcast(bf16[]{:T(256)} %constant.146.clone.1), dimensions={} | broadcast | bytes 8388610 | tf_op jit(solution)/shard_map/broadcast_in_dim | solution.py:127
  19.1 1.5 bitcast_dynamic-update-slice_fusion.7
  20.6 42.1 %collective-permute-start.2 = (bf16[256,2048]{1,0:T(8,128)(2,1)S(1)}, bf16[256,2048]{1,0:T(8,128)(2,1)}, u32[]{:S(2)}, u32[]{:S(2)}) collective-permute-start(bf16[256,2048]{1,0:T(8,128)(2,1)S(1)} %get-tuple-element.56), channel_id=1, source_target_pairs={{0,2},{1,3},{2,0},{3,1},{4,6},{5,7},{6,4},{7,5},{8,10},{9,11},{10,... | collective-permute-start | bytes 3145736 | tf_op jit(solution)/shard_map/ppermute | solution.py:122
  63.2 2.5 dynamic-slice_bitcast_fusion.2
  65.7 4.7 %dynamic-slice_bitcast_fusion = (bf16[1024,1024]{1,0:T(8,128)(2,1)}, bf16[1024,1024]{1,0:T(8,128)(2,1)}) fusion(bf16[1024,1,2048]{2,0,1:T(8,128)(2,1)} %get-tuple-element.57, s32[]{:T(128)S(6)} %select_n.199, s32[]{:T(128)S(6)} %select_n.202), kind=kLoop, calls=%fused_computation.67 | loop fusion | bytes 8388616 | tf_op jit(solution)/shard_map/dynamic_slice | solution.py:93
  70.4 5.2 %collective-permute-done.2 = bf16[256,2048]{1,0:T(8,128)(2,1)} collective-permute-done((bf16[256,2048]{1,0:T(8,128)(2,1)S(1)}, bf16[256,2048]{1,0:T(8,128)(2,1)}, u32[]{:S(2)}, u32[]{:S(2)}) %collective-permute-start.2) | collective-permute-done | bytes 1048608 | tf_op jit(solution)/shard_map/ppermute | solution.py:122
  75.5 8.4 %collective-permute-done.5 = bf16[256,2048]{1,0:T(8,128)(2,1)S(1)} collective-permute-done((bf16[256,2048]{1,0:T(8,128)(2,1)S(1)}, bf16[256,2048]{1,0:T(8,128)(2,1)S(1)}, u32[]{:S(2)}, u32[]{:S(2)}) %collective-permute-start.5) | collective-permute-done | bytes 1048608 | tf_op jit(solution)/shard_map/ppermute | solution.py:90
  84.4 19.4 %collective-permute-start.7 = (bf16[256,2048]{1,0:T(8,128)(2,1)S(1)}, bf16[256,2048]{1,0:T(8,128)(2,1)S(1)}, u32[]{:S(2)}, u32[]{:S(2)}) collective-permute-start(bf16[256,2048]{1,0:T(8,128)(2,1)S(1)} %maximum_select_fusion.1), channel_id=1, source_target_pairs={{0,2},{1,3},{2,0},{3,1},{4,6},{5,7},{6,4},{7,5},{8,10},{9,11},{10,... | collective-permute-start | bytes 3145736 | tf_op jit(solution)/shard_map/ppermute | solution.py:122
  103.7 2.4 bitcast_dynamic-update-slice_fusion.6
  106.2 2.3 bitcast_dynamic-update-slice_fusion.5
  108.5 1.5 collective-permute-start.9
  111.1 5.4 %collective-permute-done.7 = bf16[256,2048]{1,0:T(8,128)(2,1)S(1)} collective-permute-done((bf16[256,2048]{1,0:T(8,128)(2,1)S(1)}, bf16[256,2048]{1,0:T(8,128)(2,1)S(1)}, u32[]{:S(2)}, u32[]{:S(2)}) %collective-permute-start.7) | collective-permute-done | bytes 1048608 | tf_op jit(solution)/shard_map/ppermute | solution.py:122
  120.8 35.7 %collective-permute-done.9 = bf16[1024,1024]{1,0:T(8,128)(2,1)S(1)} collective-permute-done((bf16[1024,1024]{1,0:T(8,128)(2,1)S(1)}, bf16[1024,1024]{1,0:T(8,128)(2,1)S(1)}, u32[]{:S(2)}, u32[]{:S(2)}) %collective-permute-start.9) | collective-permute-done | bytes 2097184 | tf_op jit(solution)/shard_map/ppermute | solution.py:90
  156.5 5.8 %fusion.63 = bf16[512,1024]{1,0:T(8,128)(2,1)} fusion(bf16[4,512,2048]{2,1,0:T(8,128)(2,1)} %bitcast.12, s32[]{:T(128)S(6)} %select_n.222, bf16[1024,1024]{1,0:T(8,128)(2,1)S(1)} %collective-permute-done.9, bf16[1024,1024]{1,0:T(8,128)(2,1)S(1)} %copy-done.4), kind=kOutput, calls=%fused_computation.93 | convolution fusion | flops 2156396544 | bytes 7340036 | tf_op jit(solution)/shard_map/dot_general | solution.py:149
  162.3 24.0 %collective-permute-start.10 = (bf16[512,1024]{1,0:T(8,128)(2,1)}, bf16[512,1024]{1,0:T(8,128)(2,1)}, u32[]{:S(2)}, u32[]{:S(2)}) collective-permute-start(bf16[512,1024]{1,0:T(8,128)(2,1)} %fusion.63), channel_id=1, source_target_pairs={{0,8},{4,12},{24,16},{28,20},{1,9},{5,13},{25,17},{29,21},{2,10},{... | collective-permute-start | bytes 3145736 | tf_op jit(solution)/shard_map/ppermute | solution.py:155
  186.3 1.6 collective-permute-start.16
  187.9 5.6 %fusion.66 = bf16[512,1024]{1,0:T(8,128)(2,1)} fusion(bf16[4,512,2048]{2,1,0:T(8,128)(2,1)} %bitcast.12, s32[]{:T(128)S(6)} %select_n.222, bf16[1024,1024]{1,0:T(8,128)(2,1)} %collective-permute-done.4, bf16[1024,1024]{1,0:T(8,128)(2,1)S(1)} %copy-done.3), kind=kOutput, calls=%fused_computation.94 | convolution fusion | flops 2156396544 | bytes 7340036 | tf_op jit(solution)/shard_map/dot_general | solution.py:149
  193.5 2.3 collective-permute-start.15
  195.8 13.4 %collective-permute-done.10 = bf16[512,1024]{1,0:T(8,128)(2,1)} collective-permute-done((bf16[512,1024]{1,0:T(8,128)(2,1)}, bf16[512,1024]{1,0:T(8,128)(2,1)}, u32[]{:S(2)}, u32[]{:S(2)}) %collective-permute-start.10) | collective-permute-done | bytes 1048608 | tf_op jit(solution)/shard_map/ppermute | solution.py:155
  209.2 5.4 %add_convert_fusion.8 = bf16[512,1024]{1,0:T(8,128)(2,1)S(1)} fusion(bf16[512,1024]{1,0:T(8,128)(2,1)} %collective-permute-done.10, bf16[4,512,2048]{2,1,0:T(8,128)(2,1)} %bitcast.12, s32[]{:T(128)S(6)} %select_n.220, bf16[1024,1024]{1,0:T(8,128)(2,1)} %copy-done.12, bf16[1024,1024]{1,0:T(8,128)(2,1)} %get-tuple-element.60), kind=kOutput, calls=%fused_computation.82 | convolution fusion | flops 2157445120 | bytes 8388612 | tf_op jit(solution)/shard_map/dot_general | solution.py:149
  214.7 4.5 %collective-permute-start.11 = (bf16[512,1024]{1,0:T(8,128)(2,1)S(1)}, bf16[512,1024]{1,0:T(8,128)(2,1)S(1)}, u32[]{:S(2)}, u32[]{:S(2)}) collective-permute-start(bf16[512,1024]{1,0:T(8,128)(2,1)S(1)} %add_convert_fusion.8), channel_id=1, source_target_pairs={{0,8},{4,12},{8,16},{12,20},{1,9},{5,13},{9,17},{13,21},{2,10},{6,... | collective-permute-start | bytes 3145736 | tf_op jit(solution)/shard_map/ppermute | solution.py:155
  220.2 11.5 %collective-permute-done.15 = bf16[512,1024]{1,0:T(8,128)(2,1)} collective-permute-done((bf16[512,1024]{1,0:T(8,128)(2,1)}, bf16[512,1024]{1,0:T(8,128)(2,1)}, u32[]{:S(2)}, u32[]{:S(2)}) %collective-permute-start.15) | collective-permute-done | bytes 1048608 | tf_op jit(solution)/shard_map/ppermute | solution.py:155
  231.7 4.8 %add_convert_fusion.5 = bf16[512,1024]{1,0:T(8,128)(2,1)S(1)} fusion(bf16[512,1024]{1,0:T(8,128)(2,1)} %collective-permute-done.15, bf16[4,512,2048]{2,1,0:T(8,128)(2,1)} %bitcast.12, s32[]{:T(128)S(6)} %select_n.220, bf16[1024,1024]{1,0:T(8,128)(2,1)} %collective-permute-done.4, bf16[1024,1024]{1,0:T(8,128)(2,1)S(1)} %copy-done.3), kind=kOutput, calls=%fused_computation.74 | convolution fusion | flops 2157445120 | bytes 8388612 | tf_op jit(solution)/shard_map/dot_general | solution.py:149
  236.6 4.5 %collective-permute-start.17 = (bf16[512,1024]{1,0:T(8,128)(2,1)S(1)}, bf16[512,1024]{1,0:T(8,128)(2,1)S(1)}, u32[]{:S(2)}, u32[]{:S(2)}) collective-permute-start(bf16[512,1024]{1,0:T(8,128)(2,1)S(1)} %add_convert_fusion.5), channel_id=1, source_target_pairs={{0,8},{4,12},{8,16},{12,20},{1,9},{5,13},{9,17},{13,21},{2,10},{6,... | collective-permute-start | bytes 3145736 | tf_op jit(solution)/shard_map/ppermute | solution.py:155
  241.8 4.7 %fusion.69 = bf16[512,1024]{1,0:T(8,128)(2,1)S(1)} fusion(bf16[4,512,2048]{2,1,0:T(8,128)(2,1)} %bitcast.12, s32[]{:T(128)S(6)} %select_n.222, bf16[1024,1024]{1,0:T(8,128)(2,1)} %collective-permute-done.16, bf16[1024,1024]{1,0:T(8,128)(2,1)S(1)} %copy-done.6), kind=kOutput, calls=%fused_computation.95 | convolution fusion | flops 2156396544 | bytes 7340036 | tf_op jit(solution)/shard_map/dot_general | solution.py:149
  246.5 3.0 collective-permute-start.21
  249.6 4.5 %collective-permute-done.11 = bf16[512,1024]{1,0:T(8,128)(2,1)S(1)} collective-permute-done((bf16[512,1024]{1,0:T(8,128)(2,1)S(1)}, bf16[512,1024]{1,0:T(8,128)(2,1)S(1)}, u32[]{:S(2)}, u32[]{:S(2)}) %collective-permute-start.11) | collective-permute-done | bytes 1048608 | tf_op jit(solution)/shard_map/ppermute | solution.py:155
  254.1 4.0 add_convert_fusion.7
  258.1 4.0 add_convert_fusion.6
  262.1 1.3 collective-permute-start.14
  263.4 5.1 %collective-permute-start.13 = (bf16[512,1024]{1,0:T(8,128)(2,1)S(1)}, bf16[512,1024]{1,0:T(8,128)(2,1)S(1)}, u32[]{:S(2)}, u32[]{:S(2)}) collective-permute-start(bf16[512,1024]{1,0:T(8,128)(2,1)S(1)} %add_convert_fusion.7), channel_id=1, source_target_pairs={{0,8},{4,12},{8,16},{12,20},{16,24},{20,28},{1,9},{5,13},{9,17},{1... | collective-permute-start | bytes 3145736 | tf_op jit(solution)/shard_map/ppermute | solution.py:155
  268.4 4.0 fusion.30
  272.4 26.6 %collective-permute-done.21 = bf16[512,1024]{1,0:T(8,128)(2,1)S(1)} collective-permute-done((bf16[512,1024]{1,0:T(8,128)(2,1)S(1)}, bf16[512,1024]{1,0:T(8,128)(2,1)S(1)}, u32[]{:S(2)}, u32[]{:S(2)}) %collective-permute-start.21) | collective-permute-done | bytes 1048608 | tf_op jit(solution)/shard_map/ppermute | solution.py:155
  299.0 4.6 %add_convert_fusion.2 = bf16[512,1024]{1,0:T(8,128)(2,1)S(1)} fusion(bf16[512,1024]{1,0:T(8,128)(2,1)S(1)} %collective-permute-done.21, bf16[4,512,2048]{2,1,0:T(8,128)(2,1)} %bitcast.12, s32[]{:T(128)S(6)} %select_n.220, bf16[1024,1024]{1,0:T(8,128)(2,1)} %collective-permute-done.16, bf16[1024,1024]{1,0:T(8,128)(2,1)S(1)} %copy-done.6), kind=kOutput, calls=%fused_computation.66 | convolution fusion | flops 2157445120 | bytes 8388612 | tf_op jit(solution)/shard_map/dot_general | solution.py:149
  303.6 4.5 %collective-permute-start.22 = (bf16[512,1024]{1,0:T(8,128)(2,1)S(1)}, bf16[512,1024]{1,0:T(8,128)(2,1)S(1)}, u32[]{:S(2)}, u32[]{:S(2)}) collective-permute-start(bf16[512,1024]{1,0:T(8,128)(2,1)S(1)} %add_convert_fusion.2), channel_id=1, source_target_pairs={{0,8},{4,12},{8,16},{12,20},{1,9},{5,13},{9,17},{13,21},{2,10},{6,... | collective-permute-start | bytes 3145736 | tf_op jit(solution)/shard_map/ppermute | solution.py:155
  309.0 4.6 %add_convert_fusion.4 = bf16[512,1024]{1,0:T(8,128)(2,1)S(1)} fusion(bf16[512,1024]{1,0:T(8,128)(2,1)S(1)} %collective-permute-done.17, bf16[4,512,2048]{2,1,0:T(8,128)(2,1)} %bitcast.12, s32[]{:T(128)S(6)} %select_n.227, bf16[1024,1024]{1,0:T(8,128)(2,1)} %collective-permute-done.4, bf16[1024,1024]{1,0:T(8,128)(2,1)S(1)} %copy-done.3), kind=kOutput, calls=%fused_computation.72 | convolution fusion | flops 2157445120 | bytes 8388612 | tf_op jit(solution)/shard_map/dot_general | solution.py:149
  313.6 4.6 %add_convert_fusion.3 = bf16[512,1024]{1,0:T(8,128)(2,1)S(1)} fusion(bf16[512,1024]{1,0:T(8,128)(2,1)S(1)} %collective-permute-done.18, bf16[4,512,2048]{2,1,0:T(8,128)(2,1)} %bitcast.12, s32[]{:T(128)S(6)} %select_n.230, bf16[1024,1024]{1,0:T(8,128)(2,1)} %collective-permute-done.4, bf16[1024,1024]{1,0:T(8,128)(2,1)S(1)} %copy-done.3), kind=kOutput, calls=%fused_computation.70 | convolution fusion | flops 2157445120 | bytes 8388612 | tf_op jit(solution)/shard_map/dot_general | solution.py:149
  318.2 1.3 collective-permute-start.20
  319.5 4.6 %fusion.24 = f32[512,1024]{1,0:T(8,128)S(1)} fusion(bf16[4,512,2048]{2,1,0:T(8,128)(2,1)} %bitcast.12, s32[]{:T(128)S(6)} %select_n.231, bf16[1024,1024]{1,0:T(8,128)(2,1)} %collective-permute-done.4, bf16[1024,1024]{1,0:T(8,128)(2,1)S(1)} %copy-done.3), kind=kOutput, calls=%fused_computation.36 | convolution fusion | flops 2155872256 | bytes 8388612 | tf_op jit(solution)/shard_map/dot_general | solution.py:149
  324.1 4.6 %collective-permute-start.19 = (bf16[512,1024]{1,0:T(8,128)(2,1)S(1)}, bf16[512,1024]{1,0:T(8,128)(2,1)S(1)}, u32[]{:S(2)}, u32[]{:S(2)}) collective-permute-start(bf16[512,1024]{1,0:T(8,128)(2,1)S(1)} %add_convert_fusion.4), channel_id=1, source_target_pairs={{0,8},{4,12},{8,16},{12,20},{16,24},{20,28},{1,9},{5,13},{9,17},{1... | collective-permute-start | bytes 3145736 | tf_op jit(solution)/shard_map/ppermute | solution.py:155
  329.3 14.6 %collective-permute-done.22 = bf16[512,1024]{1,0:T(8,128)(2,1)S(1)} collective-permute-done((bf16[512,1024]{1,0:T(8,128)(2,1)S(1)}, bf16[512,1024]{1,0:T(8,128)(2,1)S(1)}, u32[]{:S(2)}, u32[]{:S(2)}) %collective-permute-start.22) | collective-permute-done | bytes 1048608 | tf_op jit(solution)/shard_map/ppermute | solution.py:155
  343.9 4.6 %add_convert_fusion.1 = bf16[512,1024]{1,0:T(8,128)(2,1)S(1)} fusion(bf16[512,1024]{1,0:T(8,128)(2,1)S(1)} %collective-permute-done.22, bf16[4,512,2048]{2,1,0:T(8,128)(2,1)} %bitcast.12, s32[]{:T(128)S(6)} %select_n.227, bf16[1024,1024]{1,0:T(8,128)(2,1)} %collective-permute-done.16, bf16[1024,1024]{1,0:T(8,128)(2,1)S(1)} %copy-done.6), kind=kOutput, calls=%fused_computation.64 | convolution fusion | flops 2157445120 | bytes 8388612 | tf_op jit(solution)/shard_map/dot_general | solution.py:149
  348.5 4.6 %add_convert_fusion = bf16[512,1024]{1,0:T(8,128)(2,1)S(1)} fusion(bf16[512,1024]{1,0:T(8,128)(2,1)S(1)} %collective-permute-done.23, bf16[4,512,2048]{2,1,0:T(8,128)(2,1)} %bitcast.12, s32[]{:T(128)S(6)} %select_n.230, bf16[1024,1024]{1,0:T(8,128)(2,1)} %collective-permute-done.16, bf16[1024,1024]{1,0:T(8,128)(2,1)S(1)} %copy-done.6), kind=kOutput, calls=%fused_computation.62 | convolution fusion | flops 2157445120 | bytes 8388612 | tf_op jit(solution)/shard_map/dot_general | solution.py:149
  353.1 1.3 collective-permute-start.25
  354.4 5.3 %collective-permute-start.24 = (bf16[512,1024]{1,0:T(8,128)(2,1)S(1)}, bf16[512,1024]{1,0:T(8,128)(2,1)S(1)}, u32[]{:S(2)}, u32[]{:S(2)}) collective-permute-start(bf16[512,1024]{1,0:T(8,128)(2,1)S(1)} %add_convert_fusion.1), channel_id=1, source_target_pairs={{0,8},{4,12},{8,16},{12,20},{16,24},{20,28},{1,9},{5,13},{9,17},{1... | collective-permute-start | bytes 3145736 | tf_op jit(solution)/shard_map/ppermute | solution.py:155
  359.8 6.6 %collective-permute-done.19 = bf16[512,1024]{1,0:T(8,128)(2,1)S(1)} collective-permute-done((bf16[512,1024]{1,0:T(8,128)(2,1)S(1)}, bf16[512,1024]{1,0:T(8,128)(2,1)S(1)}, u32[]{:S(2)}, u32[]{:S(2)}) %collective-permute-start.19) | collective-permute-done | bytes 1048608 | tf_op jit(solution)/shard_map/ppermute | solution.py:155
  366.9 4.6 %fusion.18 = f32[512,1024]{1,0:T(8,128)S(1)} fusion(bf16[4,512,2048]{2,1,0:T(8,128)(2,1)} %bitcast.12, s32[]{:T(128)S(6)} %select_n.231, bf16[1024,1024]{1,0:T(8,128)(2,1)} %collective-permute-done.16, bf16[1024,1024]{1,0:T(8,128)(2,1)S(1)} %copy-done.6), kind=kOutput, calls=%fused_computation.30 | convolution fusion | flops 2155872256 | bytes 8388612 | tf_op jit(solution)/shard_map/dot_general | solution.py:149
  371.5 6.8 %collective-permute-done.25 = bf16[512,1024]{1,0:T(8,128)(2,1)S(1)} collective-permute-done((bf16[512,1024]{1,0:T(8,128)(2,1)S(1)}, bf16[512,1024]{1,0:T(8,128)(2,1)S(1)}, u32[]{:S(2)}, u32[]{:S(2)}) %collective-permute-start.25) | collective-permute-done | bytes 1048608 | tf_op jit(solution)/shard_map/ppermute | solution.py:155
  378.3 9.2 %collective-permute-done.24 = bf16[512,1024]{1,0:T(8,128)(2,1)S(1)} collective-permute-done((bf16[512,1024]{1,0:T(8,128)(2,1)S(1)}, bf16[512,1024]{1,0:T(8,128)(2,1)S(1)}, u32[]{:S(2)}, u32[]{:S(2)}) %collective-permute-start.24) | collective-permute-done | bytes 1048608 | tf_op jit(solution)/shard_map/ppermute | solution.py:155
  388.1 1.3 copy-done.2
  389.4 4.4 %collective-permute-start.26 = (f32[3,2,1024]{2,1,0:T(2,128)S(1)}, f32[3,2,1024]{2,1,0:T(2,128)S(1)}, u32[]{:S(2)}, u32[]{:S(2)}) collective-permute-start(f32[3,2,1024]{2,1,0:T(2,128)S(1)} %pad_maximum_fusion.6), channel_id=1, source_target_pairs={{0,8},{4,12},{8,16},{12,20},{16,24},{20,28},{1,9},{5,13},{9,17},{1... | collective-permute-start | bytes 73736 | tf_op jit(solution)/shard_map/ppermute | solution.py:84
  393.9 1.4 collective-permute-done.26
  395.3 6.5 %fusion.10 = f32[64,8,8,128]{3,1,2,0:T(8,128)S(1)} fusion(f32[2,1024]{1,0:T(2,128)S(1)} %get-tuple-element.84, f32[512,1024]{1,0:T(8,128)} %copy-done.2, f32[2,1024]{1,0:T(2,128)S(1)} %get-tuple-element.85, f32[512,1024]{1,0:T(8,128)} %copy-done.1, f32[1024]{0:T(1024)S(1)} %bitcast.167, f32[1024]{0:T(1024)S(1)} %bitcast.168, f32[1024]{0:T(1024)S(1)} %bitcast.169, ...), kind=kLoop, calls=%fused_computation.19 | loop fusion | flops 7864320 | bytes 6332416
  402.3 2.4 shard_map.64
  404.7 3.5 collective-permute-start.29
  408.1 1.3 collective-permute-start.28
  409.4 2.5 collective-permute-start.27
  413.8 5.2 %shard_map.65 = f32[512,8,128]{2,1,0:T(8,128)S(1)} custom-call(f32[512,8,128]{2,1,0:T(8,128)S(1)} %bitcast.159, f32[512,8,128]{2,1,0:T(8,128)S(1)} %bitcast.160, f32[16,8,128]{2,1,0:T(8,128)S(1)} %bitcast.162, f32[16,8,128]{2,1,0:T(8,128)S(1)} %bitcast.163, f32[8,128]{1,0:T(8,128)S(1)} %dynamic-slice_bitcast_fusion.8.skip_ref, ...), custom_call_target="tpu_custom_call" | custom-call | tf_op jit(solution)/shard_map/pallas_call | solution.py:208
  419.7 1.8 collective-permute-start.30
  421.6 8.9 %collective-permute-done.30 = bf16[256,1024]{1,0:T(8,128)(2,1)S(1)} collective-permute-done((bf16[256,1024]{1,0:T(8,128)(2,1)S(1)}, bf16[256,1024]{1,0:T(8,128)(2,1)S(1)}, u32[]{:S(2)}, u32[]{:S(2)}) %collective-permute-start.30) | collective-permute-done | bytes 524320 | tf_op jit(solution)/shard_map/ppermute | solution.py:90
  (87 shorter events, 14.9 us)
Async XLA Ops:
  0.0 393.8 %copy-start = (f32[2048]{0:T(1024)S(1)}, f32[2048]{0:T(1024)}, u32[]{:S(2)}) copy-start(f32[2048]{0:T(1024)} %param.11) | copy-start | bytes 24580
  0.0 11.6 %collective-permute-start = (bf16[256,2048]{1,0:T(8,128)(2,1)}, bf16[256,2048]{1,0:T(8,128)(2,1)S(1)}, u32[]{:S(2)}, u32[]{:S(2)}) collective-permute-start(bf16[256,2048]{1,0:T(8,128)(2,1)} %param.6), channel_id=1, source_target_pairs={{0,0},{1,8},{2,16},{3,24},{4,4},{5,12},{6,20},{7,28},{8,1},{9,9},{... | collective-permute-start | bytes 3145736 | tf_op jit(solution)/shard_map/ppermute | solution.py:107
  11.7 72.6 %collective-permute-start.4 = (bf16[1024,1024]{1,0:T(8,128)(2,1)}, bf16[1024,1024]{1,0:T(8,128)(2,1)}, u32[]{:S(2)}, u32[]{:S(2)}) collective-permute-start(bf16[1024,1024]{1,0:T(8,128)(2,1)} %get-tuple-element.31), channel_id=1, source_target_pairs={{0,4},{4,0},{8,12},{12,8},{16,20},{20,16},{24,28},{28,24},{1,5},{5... | collective-permute-start | bytes 6291464 | tf_op jit(solution)/shard_map/ppermute | solution.py:90
  20.6 54.9 %collective-permute-start.2 = (bf16[256,2048]{1,0:T(8,128)(2,1)S(1)}, bf16[256,2048]{1,0:T(8,128)(2,1)}, u32[]{:S(2)}, u32[]{:S(2)}) collective-permute-start(bf16[256,2048]{1,0:T(8,128)(2,1)S(1)} %get-tuple-element.56), channel_id=1, source_target_pairs={{0,2},{1,3},{2,0},{3,1},{4,6},{5,7},{6,4},{7,5},{8,10},{9,11},{10,... | collective-permute-start | bytes 3145736 | tf_op jit(solution)/shard_map/ppermute | solution.py:122
  62.7 21.2 %collective-permute-start.5 = (bf16[256,2048]{1,0:T(8,128)(2,1)S(1)}, bf16[256,2048]{1,0:T(8,128)(2,1)S(1)}, u32[]{:S(2)}, u32[]{:S(2)}) collective-permute-start(bf16[256,2048]{1,0:T(8,128)(2,1)S(1)} %collective-permute-done), channel_id=1, source_target_pairs={{0,4},{4,0},{8,12},{12,8},{16,20},{20,16},{24,28},{28,24},{1,5},{5... | collective-permute-start | bytes 3145736 | tf_op jit(solution)/shard_map/ppermute | solution.py:90
  63.2 40.5 %collective-permute-start.1 = (bf16[256,2048]{1,0:T(8,128)(2,1)S(1)}, bf16[256,2048]{1,0:T(8,128)(2,1)}, u32[]{:S(2)}, u32[]{:S(2)}) collective-permute-start(bf16[256,2048]{1,0:T(8,128)(2,1)S(1)} %get-tuple-element.56), channel_id=1, source_target_pairs={{0,1},{1,0},{2,3},{3,2},{4,5},{5,4},{6,7},{7,6},{8,9},{9,8},{10,11... | collective-permute-start | bytes 3145736 | tf_op jit(solution)/shard_map/ppermute | solution.py:125
  75.5 34.5 %collective-permute-start.3 = (bf16[256,2048]{1,0:T(8,128)(2,1)}, bf16[256,2048]{1,0:T(8,128)(2,1)S(1)}, u32[]{:S(2)}, u32[]{:S(2)}) collective-permute-start(bf16[256,2048]{1,0:T(8,128)(2,1)} %collective-permute-done.2), channel_id=1, source_target_pairs={{0,1},{1,0},{2,3},{3,2},{4,5},{5,4},{6,7},{7,6},{8,9},{9,8},{10,11... | collective-permute-start | bytes 3145736 | tf_op jit(solution)/shard_map/ppermute | solution.py:125
  84.4 32.1 %collective-permute-start.7 = (bf16[256,2048]{1,0:T(8,128)(2,1)S(1)}, bf16[256,2048]{1,0:T(8,128)(2,1)S(1)}, u32[]{:S(2)}, u32[]{:S(2)}) collective-permute-start(bf16[256,2048]{1,0:T(8,128)(2,1)S(1)} %maximum_select_fusion.1), channel_id=1, source_target_pairs={{0,2},{1,3},{2,0},{3,1},{4,6},{5,7},{6,4},{7,5},{8,10},{9,11},{10,... | collective-permute-start | bytes 3145736 | tf_op jit(solution)/shard_map/ppermute | solution.py:122
  103.7 4.8 %copy-start.7 = (bf16[1024,1024]{1,0:T(8,128)(2,1)S(1)}, bf16[1024,1024]{1,0:T(8,128)(2,1)}, u32[]{:S(2)}) copy-start(bf16[1024,1024]{1,0:T(8,128)(2,1)} %get-tuple-element.33) | copy-start | bytes 6291460
  106.2 11.4 %collective-permute-start.6 = (bf16[256,2048]{1,0:T(8,128)(2,1)S(1)}, bf16[256,2048]{1,0:T(8,128)(2,1)S(1)}, u32[]{:S(2)}, u32[]{:S(2)}) collective-permute-start(bf16[256,2048]{1,0:T(8,128)(2,1)S(1)} %maximum_select_fusion.1), channel_id=1, source_target_pairs={{0,1},{1,0},{2,3},{3,2},{4,5},{5,4},{6,7},{7,6},{8,9},{9,8},{10,11... | collective-permute-start | bytes 3145736 | tf_op jit(solution)/shard_map/ppermute | solution.py:125
  108.5 48.0 %collective-permute-start.9 = (bf16[1024,1024]{1,0:T(8,128)(2,1)S(1)}, bf16[1024,1024]{1,0:T(8,128)(2,1)S(1)}, u32[]{:S(2)}, u32[]{:S(2)}) collective-permute-start(bf16[1024,1024]{1,0:T(8,128)(2,1)S(1)} %copy-done.7), channel_id=1, source_target_pairs={{0,4},{4,0},{8,12},{12,8},{16,20},{20,16},{24,28},{28,24},{1,5},{5... | collective-permute-start | bytes 6291464 | tf_op jit(solution)/shard_map/ppermute | solution.py:90
  116.5 3.2 collective-permute-start.8
  118.6 37.9 %copy-start.4 = (bf16[1024,1024]{1,0:T(8,128)(2,1)S(1)}, bf16[1024,1024]{1,0:T(8,128)(2,1)}, u32[]{:S(2)}) copy-start(bf16[1024,1024]{1,0:T(8,128)(2,1)} %get-tuple-element.60) | copy-start | bytes 6291460
  156.5 5.8 %copy-start.12 = (bf16[1024,1024]{1,0:T(8,128)(2,1)}, bf16[1024,1024]{1,0:T(8,128)(2,1)S(1)}, u32[]{:S(2)}) copy-start(bf16[1024,1024]{1,0:T(8,128)(2,1)S(1)} %collective-permute-done.9) | copy-start | bytes 6291460
  156.5 31.4 %copy-start.3 = (bf16[1024,1024]{1,0:T(8,128)(2,1)S(1)}, bf16[1024,1024]{1,0:T(8,128)(2,1)}, u32[]{:S(2)}) copy-start(bf16[1024,1024]{1,0:T(8,128)(2,1)} %get-tuple-element.64) | copy-start | bytes 6291460
  162.3 46.9 %collective-permute-start.10 = (bf16[512,1024]{1,0:T(8,128)(2,1)}, bf16[512,1024]{1,0:T(8,128)(2,1)}, u32[]{:S(2)}, u32[]{:S(2)}) collective-permute-start(bf16[512,1024]{1,0:T(8,128)(2,1)} %fusion.63), channel_id=1, source_target_pairs={{0,8},{4,12},{24,16},{28,20},{1,9},{5,13},{25,17},{29,21},{2,10},{... | collective-permute-start | bytes 3145736 | tf_op jit(solution)/shard_map/ppermute | solution.py:155
  186.3 50.2 %collective-permute-start.16 = (bf16[1024,1024]{1,0:T(8,128)(2,1)}, bf16[1024,1024]{1,0:T(8,128)(2,1)}, u32[]{:S(2)}, u32[]{:S(2)}) collective-permute-start(bf16[1024,1024]{1,0:T(8,128)(2,1)} %get-tuple-element.42), channel_id=1, source_target_pairs={{0,4},{4,0},{8,12},{12,8},{16,20},{20,16},{24,28},{28,24},{1,5},{5... | collective-permute-start | bytes 6291464 | tf_op jit(solution)/shard_map/ppermute | solution.py:90
  187.9 7.8 %copy-start.11 = (bf16[3,3,2048]{2,1,0:T(4,128)(2,1)S(1)}, bf16[3,3,2048]{2,1,0:T(4,128)(2,1)}, u32[]{:S(2)}) copy-start(bf16[3,3,2048]{2,1,0:T(4,128)(2,1)} %param.8) | copy-start | bytes 110596
  193.5 38.2 %collective-permute-start.15 = (bf16[512,1024]{1,0:T(8,128)(2,1)}, bf16[512,1024]{1,0:T(8,128)(2,1)}, u32[]{:S(2)}, u32[]{:S(2)}) collective-permute-start(bf16[512,1024]{1,0:T(8,128)(2,1)} %fusion.66), channel_id=1, source_target_pairs={{0,8},{4,12},{24,16},{28,20},{1,9},{5,13},{25,17},{29,21},{2,10},{... | collective-permute-start | bytes 3145736 | tf_op jit(solution)/shard_map/ppermute | solution.py:155
  195.8 23.3 %copy-start.9 = (f32[2048,16]{0,1:T(8,128)S(1)}, f32[2048,16]{0,1:T(8,128)}, u32[]{:S(2)}) copy-start(f32[2048,16]{0,1:T(8,128)} %param.9) | copy-start | bytes 393220
  195.8 23.3 %copy-start.10 = (f32[2048,16]{0,1:T(8,128)S(1)}, f32[2048,16]{0,1:T(8,128)}, u32[]{:S(2)}) copy-start(f32[2048,16]{0,1:T(8,128)} %param.10) | copy-start | bytes 393220
  214.7 39.4 %collective-permute-start.11 = (bf16[512,1024]{1,0:T(8,128)(2,1)S(1)}, bf16[512,1024]{1,0:T(8,128)(2,1)S(1)}, u32[]{:S(2)}, u32[]{:S(2)}) collective-permute-start(bf16[512,1024]{1,0:T(8,128)(2,1)S(1)} %add_convert_fusion.8), channel_id=1, source_target_pairs={{0,8},{4,12},{8,16},{12,20},{1,9},{5,13},{9,17},{13,21},{2,10},{6,... | collective-permute-start | bytes 3145736 | tf_op jit(solution)/shard_map/ppermute | solution.py:155
  219.2 22.6 %copy-start.6 = (bf16[1024,1024]{1,0:T(8,128)(2,1)S(1)}, bf16[1024,1024]{1,0:T(8,128)(2,1)}, u32[]{:S(2)}) copy-start(bf16[1024,1024]{1,0:T(8,128)(2,1)} %get-tuple-element.62) | copy-start | bytes 6291460
  219.2 38.8 %collective-permute-start.12 = (bf16[512,1024]{1,0:T(8,128)(2,1)S(1)}, bf16[512,1024]{1,0:T(8,128)(2,1)S(1)}, u32[]{:S(2)}, u32[]{:S(2)}) collective-permute-start(bf16[512,1024]{1,0:T(8,128)(2,1)S(1)} %add_convert_fusion.8), channel_id=1, source_target_pairs={{24,16},{28,20},{16,8},{20,12},{25,17},{29,21},{17,9},{21,13},{26,... | collective-permute-start | bytes 3145736 | tf_op jit(solution)/shard_map/ppermute | solution.py:155
  236.6 71.5 %collective-permute-start.17 = (bf16[512,1024]{1,0:T(8,128)(2,1)S(1)}, bf16[512,1024]{1,0:T(8,128)(2,1)S(1)}, u32[]{:S(2)}, u32[]{:S(2)}) collective-permute-start(bf16[512,1024]{1,0:T(8,128)(2,1)S(1)} %add_convert_fusion.5), channel_id=1, source_target_pairs={{0,8},{4,12},{8,16},{12,20},{1,9},{5,13},{9,17},{13,21},{2,10},{6,... | collective-permute-start | bytes 3145736 | tf_op jit(solution)/shard_map/ppermute | solution.py:155
  241.0 72.6 %collective-permute-start.18 = (bf16[512,1024]{1,0:T(8,128)(2,1)S(1)}, bf16[512,1024]{1,0:T(8,128)(2,1)S(1)}, u32[]{:S(2)}, u32[]{:S(2)}) collective-permute-start(bf16[512,1024]{1,0:T(8,128)(2,1)S(1)} %add_convert_fusion.5), channel_id=1, source_target_pairs={{24,16},{28,20},{16,8},{20,12},{25,17},{29,21},{17,9},{21,13},{26,... | collective-permute-start | bytes 3145736 | tf_op jit(solution)/shard_map/ppermute | solution.py:155
  241.8 12.3 %copy-start.5 = (bf16[1024,1024]{1,0:T(8,128)(2,1)S(1)}, bf16[1024,1024]{1,0:T(8,128)(2,1)}, u32[]{:S(2)}) copy-start(bf16[1024,1024]{1,0:T(8,128)(2,1)} %get-tuple-element.60) | copy-start | bytes 6291460
  241.8 12.3 %copy-start.13 = (bf16[1024,1024]{1,0:T(8,128)(2,1)S(1)}, bf16[1024,1024]{1,0:T(8,128)(2,1)}, u32[]{:S(2)}) copy-start(bf16[1024,1024]{1,0:T(8,128)(2,1)} %copy-done.12) | copy-start | bytes 6291460
  246.5 52.5 %collective-permute-start.21 = (bf16[512,1024]{1,0:T(8,128)(2,1)S(1)}, bf16[512,1024]{1,0:T(8,128)(2,1)S(1)}, u32[]{:S(2)}, u32[]{:S(2)}) collective-permute-start(bf16[512,1024]{1,0:T(8,128)(2,1)S(1)} %fusion.69), channel_id=1, source_target_pairs={{0,8},{4,12},{24,16},{28,20},{1,9},{5,13},{25,17},{29,21},{2,10},{... | collective-permute-start | bytes 3145736 | tf_op jit(solution)/shard_map/ppermute | solution.py:155
  262.1 62.1 %collective-permute-start.14 = (bf16[512,1024]{1,0:T(8,128)(2,1)S(1)}, bf16[512,1024]{1,0:T(8,128)(2,1)S(1)}, u32[]{:S(2)}, u32[]{:S(2)}) collective-permute-start(bf16[512,1024]{1,0:T(8,128)(2,1)S(1)} %add_convert_fusion.6), channel_id=1, source_target_pairs={{24,16},{28,20},{16,8},{20,12},{8,0},{12,4},{25,17},{29,21},{17,9}... | collective-permute-start | bytes 3145736 | tf_op jit(solution)/shard_map/ppermute | solution.py:155
  263.4 65.4 %collective-permute-start.13 = (bf16[512,1024]{1,0:T(8,128)(2,1)S(1)}, bf16[512,1024]{1,0:T(8,128)(2,1)S(1)}, u32[]{:S(2)}, u32[]{:S(2)}) collective-permute-start(bf16[512,1024]{1,0:T(8,128)(2,1)S(1)} %add_convert_fusion.7), channel_id=1, source_target_pairs={{0,8},{4,12},{8,16},{12,20},{16,24},{20,28},{1,9},{5,13},{9,17},{1... | collective-permute-start | bytes 3145736 | tf_op jit(solution)/shard_map/ppermute | solution.py:155
  303.6 40.4 %collective-permute-start.22 = (bf16[512,1024]{1,0:T(8,128)(2,1)S(1)}, bf16[512,1024]{1,0:T(8,128)(2,1)S(1)}, u32[]{:S(2)}, u32[]{:S(2)}) collective-permute-start(bf16[512,1024]{1,0:T(8,128)(2,1)S(1)} %add_convert_fusion.2), channel_id=1, source_target_pairs={{0,8},{4,12},{8,16},{12,20},{1,9},{5,13},{9,17},{13,21},{2,10},{6,... | collective-permute-start | bytes 3145736 | tf_op jit(solution)/shard_map/ppermute | solution.py:155
  308.1 40.5 %collective-permute-start.23 = (bf16[512,1024]{1,0:T(8,128)(2,1)S(1)}, bf16[512,1024]{1,0:T(8,128)(2,1)S(1)}, u32[]{:S(2)}, u32[]{:S(2)}) collective-permute-start(bf16[512,1024]{1,0:T(8,128)(2,1)S(1)} %add_convert_fusion.2), channel_id=1, source_target_pairs={{24,16},{28,20},{16,8},{20,12},{25,17},{29,21},{17,9},{21,13},{26,... | collective-permute-start | bytes 3145736 | tf_op jit(solution)/shard_map/ppermute | solution.py:155
  318.2 41.6 %collective-permute-start.20 = (bf16[512,1024]{1,0:T(8,128)(2,1)S(1)}, bf16[512,1024]{1,0:T(8,128)(2,1)S(1)}, u32[]{:S(2)}, u32[]{:S(2)}) collective-permute-start(bf16[512,1024]{1,0:T(8,128)(2,1)S(1)} %add_convert_fusion.3), channel_id=1, source_target_pairs={{24,16},{28,20},{16,8},{20,12},{8,0},{12,4},{25,17},{29,21},{17,9}... | collective-permute-start | bytes 3145736 | tf_op jit(solution)/shard_map/ppermute | solution.py:155
  324.1 42.3 %collective-permute-start.19 = (bf16[512,1024]{1,0:T(8,128)(2,1)S(1)}, bf16[512,1024]{1,0:T(8,128)(2,1)S(1)}, u32[]{:S(2)}, u32[]{:S(2)}) collective-permute-start(bf16[512,1024]{1,0:T(8,128)(2,1)S(1)} %add_convert_fusion.4), channel_id=1, source_target_pairs={{0,8},{4,12},{8,16},{12,20},{16,24},{20,28},{1,9},{5,13},{9,17},{1... | collective-permute-start | bytes 3145736 | tf_op jit(solution)/shard_map/ppermute | solution.py:155
  329.3 30.5 %copy-start.1 = (f32[512,1024]{1,0:T(8,128)}, f32[512,1024]{1,0:T(8,128)S(1)}, u32[]{:S(2)}) copy-start(f32[512,1024]{1,0:T(8,128)S(1)} %convert_add_fusion.2) | copy-start | bytes 6291460
  353.1 25.2 %collective-permute-start.25 = (bf16[512,1024]{1,0:T(8,128)(2,1)S(1)}, bf16[512,1024]{1,0:T(8,128)(2,1)S(1)}, u32[]{:S(2)}, u32[]{:S(2)}) collective-permute-start(bf16[512,1024]{1,0:T(8,128)(2,1)S(1)} %add_convert_fusion), channel_id=1, source_target_pairs={{24,16},{28,20},{16,8},{20,12},{8,0},{12,4},{25,17},{29,21},{17,9}... | collective-permute-start | bytes 3145736 | tf_op jit(solution)/shard_map/ppermute | solution.py:155
  354.4 33.1 %collective-permute-start.24 = (bf16[512,1024]{1,0:T(8,128)(2,1)S(1)}, bf16[512,1024]{1,0:T(8,128)(2,1)S(1)}, u32[]{:S(2)}, u32[]{:S(2)}) collective-permute-start(bf16[512,1024]{1,0:T(8,128)(2,1)S(1)} %add_convert_fusion.1), channel_id=1, source_target_pairs={{0,8},{4,12},{8,16},{12,20},{16,24},{20,28},{1,9},{5,13},{9,17},{1... | collective-permute-start | bytes 3145736 | tf_op jit(solution)/shard_map/ppermute | solution.py:155
  388.1 1.3 copy-start.2
  389.4 5.9 %collective-permute-start.26 = (f32[3,2,1024]{2,1,0:T(2,128)S(1)}, f32[3,2,1024]{2,1,0:T(2,128)S(1)}, u32[]{:S(2)}, u32[]{:S(2)}) collective-permute-start(f32[3,2,1024]{2,1,0:T(2,128)S(1)} %pad_maximum_fusion.6), channel_id=1, source_target_pairs={{0,8},{4,12},{8,16},{12,20},{16,24},{20,28},{1,9},{5,13},{9,17},{1... | collective-permute-start | bytes 73736 | tf_op jit(solution)/shard_map/ppermute | solution.py:84
  404.7 8.4 %collective-permute-start.29 = (f32[16,8,128]{2,1,0:T(8,128)S(1)}, f32[16,8,128]{2,1,0:T(8,128)S(1)}, u32[]{:S(2)}, u32[]{:S(2)}) collective-permute-start(f32[16,8,128]{2,1,0:T(8,128)S(1)} %shard_map.64), channel_id=1, source_target_pairs={{0,24},{4,28},{1,25},{5,29},{2,26},{6,30},{3,27},{7,31}} | collective-permute-start | bytes 196616 | tf_op jit(solution)/shard_map/ppermute | solution.py:84
  408.1 4.9 %collective-permute-start.28 = (f32[16,8,128]{2,1,0:T(8,128)S(1)}, f32[16,8,128]{2,1,0:T(8,128)S(1)}, u32[]{:S(2)}, u32[]{:S(2)}) collective-permute-start(f32[16,8,128]{2,1,0:T(8,128)S(1)} %shard_map.64), channel_id=1, source_target_pairs={{0,16},{4,20},{8,24},{12,28},{1,17},{5,21},{9,25},{13,29},{2,18},{... | collective-permute-start | bytes 196616 | tf_op jit(solution)/shard_map/ppermute | solution.py:84
  409.4 4.4 %collective-permute-start.27 = (f32[16,8,128]{2,1,0:T(8,128)S(1)}, f32[16,8,128]{2,1,0:T(8,128)S(1)}, u32[]{:S(2)}, u32[]{:S(2)}) collective-permute-start(f32[16,8,128]{2,1,0:T(8,128)S(1)} %shard_map.64), channel_id=1, source_target_pairs={{0,8},{4,12},{8,16},{12,20},{16,24},{20,28},{1,9},{5,13},{9,17},{1... | collective-permute-start | bytes 196616 | tf_op jit(solution)/shard_map/ppermute | solution.py:84
  419.7 10.8 %collective-permute-start.30 = (bf16[256,1024]{1,0:T(8,128)(2,1)S(1)}, bf16[256,1024]{1,0:T(8,128)(2,1)S(1)}, u32[]{:S(2)}, u32[]{:S(2)}) collective-permute-start(bf16[256,1024]{1,0:T(8,128)(2,1)S(1)} %dynamic-slice_bitcast_fusion.6), channel_id=1, source_target_pairs={{0,4},{4,0},{8,12},{12,8},{16,20},{20,16},{24,28},{28,24},{1,5},{5... | collective-permute-start | bytes 1572872 | tf_op jit(solution)/shard_map/ppermute | solution.py:90
  421.6 8.9 %copy-start.8 = (bf16[256,2048]{1,0:T(8,128)(2,1)}, bf16[256,2048]{1,0:T(8,128)(2,1)S(1)}, u32[]{:S(2)}) copy-start(bf16[256,2048]{1,0:T(8,128)(2,1)S(1)} %bitcast_dynamic-update-slice_fusion.8) | copy-start | bytes 3145732

commit v2 on v1

--- a/solution.py
+++ b/solution.py
@@ -45,6 +45,10 @@
     lax.fori_loop(0, gated_ref.shape[0] // STEPS, body, start)
 
 
+def swapped(i):
+    return (i % 2) * 2 + i // 2
+
+
 def rolled(array, x, feats, n_x):
     result = array
     for k in range(1, n_x):
@@ -98,7 +102,7 @@
         return [along_x(block, hop) for hop, block in enumerate(away[g], 1)]
 
     route = [
-        ((i * n_x + k) * n_ch + a * n_q + q, (a * n_x + k) * n_ch + i * n_q + q)
+        ((i * n_x + k) * n_ch + a * n_q + q, (a * n_x + k) * n_ch + swapped(i) * n_q + q)
         for i in range(LINE)
         for k in range(n_x)
         for a in range(LINE)
@@ -131,8 +135,9 @@
             source = (mine - step * CORES) % n_ch
             for core, piece in enumerate((block, other_core(block))):
                 owner = source + core * (1 - 2 * (mine % CORES))
+                slot = swapped(owner // n_q) * n_q + owner % n_q
                 found = lax.dynamic_update_slice(
-                    found, piece[None, None], (owner, (x - hop) % n_x, 0, 0)
+                    found, piece[None, None], (slot, (x - hop) % n_x, 0, 0)
                 )
     found, came[1], away[2] = lax.optimization_barrier((found, came[1], away[2]))
     came.append(exchange(2))

time: 440 us -> 440 us (level)
  waiting for transfers between devices: 159 us -> 146 us
  starting transfers between devices: 148 us -> 160 us
    ppermute x4, starting transfers between devices: 0.01 us -> 25.9 us  [other_core(): return lax.ppermute(block, 'ch', [(i, i ^ 1) for i in range(n_ch)])]
    ppermute x5, waiting for transfers between devices: 53 us -> 34 us  [along_x(): return lax.ppermute(block, 'ctx', route)]
    ppermute x2, starting transfers between devices: 61.4 us -> 48.8 us  [along_outer(): return lax.ppermute(block, 'ch', route)]
    ppermute x2, waiting for transfers between devices: 10.6 us -> 16.1 us  [along_outer(): return lax.ppermute(block, 'ch', route)]
  transfers between devices with their start and end apart: 31 -> 31, of which waited for: 15 -> 13; matrix products, arithmetic and copies ran while one was open for 23% -> 23% of each run, Pallas kernels for 0% -> 0%
where the time goes in v2:
time: 440 us; the launch traced here: 431 us
  starting transfers between devices  160 us (36%)
  waiting for transfers between devices  146 us (33%)
  matrix products  70.4 us (16%)
  local copies, waits for them, and re-layouts  35.3 us (8%)
  other arithmetic  10.7 us (2%)
  Pallas kernels  7.56 us (2%)
    ppermute x15, waiting for transfers between devices, hops(): lax.ppermute(block, 'ctx', [(i * n_x + k, j * n_x + k) for i, j in pairs...  93.8 us
    dot_general x15, matrix products, share(): return jnp.dot(block, weight, preferred_element_type=jnp.float32)  70.4 us
    ppermute x15, starting transfers between devices, hops(): lax.ppermute(block, 'ctx', [(i * n_x + k, j * n_x + k) for i, j in pairs...  64.6 us
    ppermute x2, starting transfers between devices, along_outer(): return lax.ppermute(block, 'ch', route)  48.8 us
    ppermute x5, waiting for transfers between devices, along_x(): return lax.ppermute(block, 'ctx', route)  34 us
    ppermute x4, starting transfers between devices, other_core(): return lax.ppermute(block, 'ch', [(i, i ^ 1) for i in range(n_ch)])  25.9 us
    ppermute x2, waiting for transfers between devices, along_outer(): return lax.ppermute(block, 'ch', route)  16.1 us
    ppermute x4, starting transfers between devices, along_z(): return lax.ppermute(block, 'ctx', route)  10.5 us
  transfers between devices with their start and end apart: 31, of which 13 were waited for; matrix products, arithmetic and copies ran while one was open for 23% of the time, Pallas kernels for 0%

profile of v2, /device:TPU:0, one launch (start us, length us, event | category | flops | bytes accessed | tf_op | source)
XLA Modules:
  0.0 431.3 jit_solution(5316537614423901821)
XLA Ops:
  0.0 2.0 collective-permute-start
  2.0 7.0 %fusion.107 = (bf16[1024,1,2048]{2,0,1:T(8,128)(2,1)}, bf16[1024,1,2048]{2,0,1:T(8,128)(2,1)S(1)}, bf16[1024,1,2048]{2,0,1:T(8,128)(2,1)S(1)}) fusion(bf16[1024,3,2048]{2,0,1:T(8,128)(2,1)} %param.7), kind=kLoop, calls=%fused_computation.144 | loop fusion | bytes 25165824 | tf_op jit(solution)/shard_map/slice | solution.py:97
  9.0 2.6 dynamic-slice_bitcast_fusion.1
  11.7 3.0 collective-permute-start.4
  14.7 4.4 %broadcast_in_dim.31 = bf16[4,2,256,2048]{3,2,1,0:T(8,128)(2,1)} broadcast(bf16[]{:T(256)} %constant.276.clone.1), dimensions={} | broadcast | bytes 8388610 | tf_op jit(solution)/shard_map/broadcast_in_dim | solution.py:131
  19.1 1.5 bitcast_dynamic-update-slice_fusion.7
  20.6 18.6 %collective-permute-start.2 = (bf16[256,2048]{1,0:T(8,128)(2,1)S(1)}, bf16[256,2048]{1,0:T(8,128)(2,1)}, u32[]{:S(2)}, u32[]{:S(2)}) collective-permute-start(bf16[256,2048]{1,0:T(8,128)(2,1)S(1)} %get-tuple-element.56), channel_id=1, source_target_pairs={{0,2},{1,3},{2,0},{3,1},{4,6},{5,7},{6,4},{7,5},{8,10},{9,11},{10,... | collective-permute-start | bytes 3145736 | tf_op jit(solution)/shard_map/ppermute | solution.py:126
  39.8 19.6 %collective-permute-start.1 = (bf16[256,2048]{1,0:T(8,128)(2,1)S(1)}, bf16[256,2048]{1,0:T(8,128)(2,1)}, u32[]{:S(2)}, u32[]{:S(2)}) collective-permute-start(bf16[256,2048]{1,0:T(8,128)(2,1)S(1)} %get-tuple-element.56), channel_id=1, source_target_pairs={{0,1},{1,0},{2,3},{3,2},{4,5},{5,4},{6,7},{7,6},{8,9},{9,8},{10,11... | collective-permute-start | bytes 3145736 | tf_op jit(solution)/shard_map/ppermute | solution.py:129
  59.4 2.5 dynamic-slice_bitcast_fusion.2
  61.8 4.7 %dynamic-slice_bitcast_fusion = (bf16[1024,1024]{1,0:T(8,128)(2,1)}, bf16[1024,1024]{1,0:T(8,128)(2,1)}) fusion(bf16[1024,1,2048]{2,0,1:T(8,128)(2,1)} %get-tuple-element.57, s32[]{:T(128)S(6)} %select_n.263, s32[]{:T(128)S(6)} %select_n.266), kind=kLoop, calls=%fused_computation.67 | loop fusion | bytes 8388616 | tf_op jit(solution)/shard_map/dynamic_slice | solution.py:97
  66.5 6.3 %collective-permute-start.3 = (bf16[256,2048]{1,0:T(8,128)(2,1)}, bf16[256,2048]{1,0:T(8,128)(2,1)S(1)}, u32[]{:S(2)}, u32[]{:S(2)}) collective-permute-start(bf16[256,2048]{1,0:T(8,128)(2,1)} %collective-permute-done.2), channel_id=1, source_target_pairs={{0,1},{1,0},{2,3},{3,2},{4,5},{5,4},{6,7},{7,6},{8,9},{9,8},{10,11... | collective-permute-start | bytes 3145736 | tf_op jit(solution)/shard_map/ppermute | solution.py:129
  73.3 30.2 %collective-permute-start.7 = (bf16[256,2048]{1,0:T(8,128)(2,1)S(1)}, bf16[256,2048]{1,0:T(8,128)(2,1)S(1)}, u32[]{:S(2)}, u32[]{:S(2)}) collective-permute-start(bf16[256,2048]{1,0:T(8,128)(2,1)S(1)} %maximum_select_fusion.1), channel_id=1, source_target_pairs={{0,2},{1,3},{2,0},{3,1},{4,6},{5,7},{6,4},{7,5},{8,10},{9,11},{10,... | collective-permute-start | bytes 3145736 | tf_op jit(solution)/shard_map/ppermute | solution.py:126
  103.5 2.5 bitcast_dynamic-update-slice_fusion.6
  106.0 2.3 bitcast_dynamic-update-slice_fusion.5
  108.3 1.5 collective-permute-start.9
  110.8 16.1 %collective-permute-done.7 = bf16[256,2048]{1,0:T(8,128)(2,1)S(1)} collective-permute-done((bf16[256,2048]{1,0:T(8,128)(2,1)S(1)}, bf16[256,2048]{1,0:T(8,128)(2,1)S(1)}, u32[]{:S(2)}, u32[]{:S(2)}) %collective-permute-start.7) | collective-permute-done | bytes 1048608 | tf_op jit(solution)/shard_map/ppermute | solution.py:126
  131.2 25.1 %collective-permute-done.9 = bf16[1024,1024]{1,0:T(8,128)(2,1)S(1)} collective-permute-done((bf16[1024,1024]{1,0:T(8,128)(2,1)S(1)}, bf16[1024,1024]{1,0:T(8,128)(2,1)S(1)}, u32[]{:S(2)}, u32[]{:S(2)}) %collective-permute-start.9) | collective-permute-done | bytes 2097184 | tf_op jit(solution)/shard_map/ppermute | solution.py:94
  156.3 5.8 %fusion.63 = bf16[512,1024]{1,0:T(8,128)(2,1)} fusion(bf16[4,512,2048]{2,1,0:T(8,128)(2,1)} %bitcast.12, s32[]{:T(128)S(6)} %select_n.294, bf16[1024,1024]{1,0:T(8,128)(2,1)S(1)} %collective-permute-done.9, bf16[1024,1024]{1,0:T(8,128)(2,1)S(1)} %copy-done.4), kind=kOutput, calls=%fused_computation.93 | convolution fusion | flops 2156396544 | bytes 7340036 | tf_op jit(solution)/shard_map/dot_general | solution.py:154
  162.1 24.9 %collective-permute-start.10 = (bf16[512,1024]{1,0:T(8,128)(2,1)}, bf16[512,1024]{1,0:T(8,128)(2,1)}, u32[]{:S(2)}, u32[]{:S(2)}) collective-permute-start(bf16[512,1024]{1,0:T(8,128)(2,1)} %fusion.63), channel_id=1, source_target_pairs={{0,8},{4,12},{24,16},{28,20},{1,9},{5,13},{25,17},{29,21},{2,10},{... | collective-permute-start | bytes 3145736 | tf_op jit(solution)/shard_map/ppermute | solution.py:160
  187.0 1.6 collective-permute-start.16
  188.5 5.6 %fusion.66 = bf16[512,1024]{1,0:T(8,128)(2,1)} fusion(bf16[4,512,2048]{2,1,0:T(8,128)(2,1)} %bitcast.12, s32[]{:T(128)S(6)} %select_n.294, bf16[1024,1024]{1,0:T(8,128)(2,1)} %collective-permute-done.4, bf16[1024,1024]{1,0:T(8,128)(2,1)S(1)} %copy-done.3), kind=kOutput, calls=%fused_computation.94 | convolution fusion | flops 2156396544 | bytes 7340036 | tf_op jit(solution)/shard_map/dot_general | solution.py:154
  194.1 2.3 collective-permute-start.15
  196.5 13.4 %collective-permute-done.10 = bf16[512,1024]{1,0:T(8,128)(2,1)} collective-permute-done((bf16[512,1024]{1,0:T(8,128)(2,1)}, bf16[512,1024]{1,0:T(8,128)(2,1)}, u32[]{:S(2)}, u32[]{:S(2)}) %collective-permute-start.10) | collective-permute-done | bytes 1048608 | tf_op jit(solution)/shard_map/ppermute | solution.py:160
  209.9 5.4 %add_convert_fusion.8 = bf16[512,1024]{1,0:T(8,128)(2,1)S(1)} fusion(bf16[512,1024]{1,0:T(8,128)(2,1)} %collective-permute-done.10, bf16[4,512,2048]{2,1,0:T(8,128)(2,1)} %bitcast.12, s32[]{:T(128)S(6)} %select_n.292, bf16[1024,1024]{1,0:T(8,128)(2,1)} %copy-done.12, bf16[1024,1024]{1,0:T(8,128)(2,1)} %get-tuple-element.60), kind=kOutput, calls=%fused_computation.82 | convolution fusion | flops 2157445120 | bytes 8388612 | tf_op jit(solution)/shard_map/dot_general | solution.py:154
  215.3 4.5 %collective-permute-start.11 = (bf16[512,1024]{1,0:T(8,128)(2,1)S(1)}, bf16[512,1024]{1,0:T(8,128)(2,1)S(1)}, u32[]{:S(2)}, u32[]{:S(2)}) collective-permute-start(bf16[512,1024]{1,0:T(8,128)(2,1)S(1)} %add_convert_fusion.8), channel_id=1, source_target_pairs={{0,8},{4,12},{8,16},{12,20},{1,9},{5,13},{9,17},{13,21},{2,10},{6,... | collective-permute-start | bytes 3145736 | tf_op jit(solution)/shard_map/ppermute | solution.py:160
  220.9 11.5 %collective-permute-done.15 = bf16[512,1024]{1,0:T(8,128)(2,1)} collective-permute-done((bf16[512,1024]{1,0:T(8,128)(2,1)}, bf16[512,1024]{1,0:T(8,128)(2,1)}, u32[]{:S(2)}, u32[]{:S(2)}) %collective-permute-start.15) | collective-permute-done | bytes 1048608 | tf_op jit(solution)/shard_map/ppermute | solution.py:160
  232.3 4.8 %add_convert_fusion.5 = bf16[512,1024]{1,0:T(8,128)(2,1)S(1)} fusion(bf16[512,1024]{1,0:T(8,128)(2,1)} %collective-permute-done.15, bf16[4,512,2048]{2,1,0:T(8,128)(2,1)} %bitcast.12, s32[]{:T(128)S(6)} %select_n.292, bf16[1024,1024]{1,0:T(8,128)(2,1)} %collective-permute-done.4, bf16[1024,1024]{1,0:T(8,128)(2,1)S(1)} %copy-done.3), kind=kOutput, calls=%fused_computation.74 | convolution fusion | flops 2157445120 | bytes 8388612 | tf_op jit(solution)/shard_map/dot_general | solution.py:154
  237.2 4.4 %collective-permute-start.17 = (bf16[512,1024]{1,0:T(8,128)(2,1)S(1)}, bf16[512,1024]{1,0:T(8,128)(2,1)S(1)}, u32[]{:S(2)}, u32[]{:S(2)}) collective-permute-start(bf16[512,1024]{1,0:T(8,128)(2,1)S(1)} %add_convert_fusion.5), channel_id=1, source_target_pairs={{0,8},{4,12},{8,16},{12,20},{1,9},{5,13},{9,17},{13,21},{2,10},{6,... | collective-permute-start | bytes 3145736 | tf_op jit(solution)/shard_map/ppermute | solution.py:160
  242.4 4.7 %fusion.69 = bf16[512,1024]{1,0:T(8,128)(2,1)S(1)} fusion(bf16[4,512,2048]{2,1,0:T(8,128)(2,1)} %bitcast.12, s32[]{:T(128)S(6)} %select_n.294, bf16[1024,1024]{1,0:T(8,128)(2,1)} %collective-permute-done.16, bf16[1024,1024]{1,0:T(8,128)(2,1)S(1)} %copy-done.7), kind=kOutput, calls=%fused_computation.95 | convolution fusion | flops 2156396544 | bytes 7340036 | tf_op jit(solution)/shard_map/dot_general | solution.py:154
  247.2 2.5 collective-permute-start.21
  249.7 5.0 %collective-permute-done.11 = bf16[512,1024]{1,0:T(8,128)(2,1)S(1)} collective-permute-done((bf16[512,1024]{1,0:T(8,128)(2,1)S(1)}, bf16[512,1024]{1,0:T(8,128)(2,1)S(1)}, u32[]{:S(2)}, u32[]{:S(2)}) %collective-permute-start.11) | collective-permute-done | bytes 1048608 | tf_op jit(solution)/shard_map/ppermute | solution.py:160
  254.7 4.0 add_convert_fusion.7
  258.7 4.0 add_convert_fusion.6
  262.7 1.3 collective-permute-start.14
  264.0 5.1 %collective-permute-start.13 = (bf16[512,1024]{1,0:T(8,128)(2,1)S(1)}, bf16[512,1024]{1,0:T(8,128)(2,1)S(1)}, u32[]{:S(2)}, u32[]{:S(2)}) collective-permute-start(bf16[512,1024]{1,0:T(8,128)(2,1)S(1)} %add_convert_fusion.7), channel_id=1, source_target_pairs={{0,8},{4,12},{8,16},{12,20},{16,24},{20,28},{1,9},{5,13},{9,17},{1... | collective-permute-start | bytes 3145736 | tf_op jit(solution)/shard_map/ppermute | solution.py:160
  269.1 4.0 fusion.30
  273.1 26.6 %collective-permute-done.21 = bf16[512,1024]{1,0:T(8,128)(2,1)S(1)} collective-permute-done((bf16[512,1024]{1,0:T(8,128)(2,1)S(1)}, bf16[512,1024]{1,0:T(8,128)(2,1)S(1)}, u32[]{:S(2)}, u32[]{:S(2)}) %collective-permute-start.21) | collective-permute-done | bytes 1048608 | tf_op jit(solution)/shard_map/ppermute | solution.py:160
  299.7 4.6 %add_convert_fusion.2 = bf16[512,1024]{1,0:T(8,128)(2,1)S(1)} fusion(bf16[512,1024]{1,0:T(8,128)(2,1)S(1)} %collective-permute-done.21, bf16[4,512,2048]{2,1,0:T(8,128)(2,1)} %bitcast.12, s32[]{:T(128)S(6)} %select_n.292, bf16[1024,1024]{1,0:T(8,128)(2,1)} %collective-permute-done.16, bf16[1024,1024]{1,0:T(8,128)(2,1)S(1)} %copy-done.7), kind=kOutput, calls=%fused_computation.66 | convolution fusion | flops 2157445120 | bytes 8388612 | tf_op jit(solution)/shard_map/dot_general | solution.py:154
  304.2 4.5 %collective-permute-start.22 = (bf16[512,1024]{1,0:T(8,128)(2,1)S(1)}, bf16[512,1024]{1,0:T(8,128)(2,1)S(1)}, u32[]{:S(2)}, u32[]{:S(2)}) collective-permute-start(bf16[512,1024]{1,0:T(8,128)(2,1)S(1)} %add_convert_fusion.2), channel_id=1, source_target_pairs={{0,8},{4,12},{8,16},{12,20},{1,9},{5,13},{9,17},{13,21},{2,10},{6,... | collective-permute-start | bytes 3145736 | tf_op jit(solution)/shard_map/ppermute | solution.py:160
  309.7 4.6 %add_convert_fusion.4 = bf16[512,1024]{1,0:T(8,128)(2,1)S(1)} fusion(bf16[512,1024]{1,0:T(8,128)(2,1)S(1)} %collective-permute-done.17, bf16[4,512,2048]{2,1,0:T(8,128)(2,1)} %bitcast.12, s32[]{:T(128)S(6)} %select_n.299, bf16[1024,1024]{1,0:T(8,128)(2,1)} %collective-permute-done.4, bf16[1024,1024]{1,0:T(8,128)(2,1)S(1)} %copy-done.3), kind=kOutput, calls=%fused_computation.72 | convolution fusion | flops 2157445120 | bytes 8388612 | tf_op jit(solution)/shard_map/dot_general | solution.py:154
  314.3 4.6 %add_convert_fusion.3 = bf16[512,1024]{1,0:T(8,128)(2,1)S(1)} fusion(bf16[512,1024]{1,0:T(8,128)(2,1)S(1)} %collective-permute-done.18, bf16[4,512,2048]{2,1,0:T(8,128)(2,1)} %bitcast.12, s32[]{:T(128)S(6)} %select_n.302, bf16[1024,1024]{1,0:T(8,128)(2,1)} %collective-permute-done.4, bf16[1024,1024]{1,0:T(8,128)(2,1)S(1)} %copy-done.3), kind=kOutput, calls=%fused_computation.70 | convolution fusion | flops 2157445120 | bytes 8388612 | tf_op jit(solution)/shard_map/dot_general | solution.py:154
  318.9 1.3 collective-permute-start.20
  320.2 4.6 %fusion.24 = f32[512,1024]{1,0:T(8,128)S(1)} fusion(bf16[4,512,2048]{2,1,0:T(8,128)(2,1)} %bitcast.12, s32[]{:T(128)S(6)} %select_n.303, bf16[1024,1024]{1,0:T(8,128)(2,1)} %collective-permute-done.4, bf16[1024,1024]{1,0:T(8,128)(2,1)S(1)} %copy-done.3), kind=kOutput, calls=%fused_computation.36 | convolution fusion | flops 2155872256 | bytes 8388612 | tf_op jit(solution)/shard_map/dot_general | solution.py:154
  324.8 4.6 %collective-permute-start.19 = (bf16[512,1024]{1,0:T(8,128)(2,1)S(1)}, bf16[512,1024]{1,0:T(8,128)(2,1)S(1)}, u32[]{:S(2)}, u32[]{:S(2)}) collective-permute-start(bf16[512,1024]{1,0:T(8,128)(2,1)S(1)} %add_convert_fusion.4), channel_id=1, source_target_pairs={{0,8},{4,12},{8,16},{12,20},{16,24},{20,28},{1,9},{5,13},{9,17},{1... | collective-permute-start | bytes 3145736 | tf_op jit(solution)/shard_map/ppermute | solution.py:160
  330.0 14.6 %collective-permute-done.22 = bf16[512,1024]{1,0:T(8,128)(2,1)S(1)} collective-permute-done((bf16[512,1024]{1,0:T(8,128)(2,1)S(1)}, bf16[512,1024]{1,0:T(8,128)(2,1)S(1)}, u32[]{:S(2)}, u32[]{:S(2)}) %collective-permute-start.22) | collective-permute-done | bytes 1048608 | tf_op jit(solution)/shard_map/ppermute | solution.py:160
  344.6 4.6 %add_convert_fusion.1 = bf16[512,1024]{1,0:T(8,128)(2,1)S(1)} fusion(bf16[512,1024]{1,0:T(8,128)(2,1)S(1)} %collective-permute-done.22, bf16[4,512,2048]{2,1,0:T(8,128)(2,1)} %bitcast.12, s32[]{:T(128)S(6)} %select_n.299, bf16[1024,1024]{1,0:T(8,128)(2,1)} %collective-permute-done.16, bf16[1024,1024]{1,0:T(8,128)(2,1)S(1)} %copy-done.7), kind=kOutput, calls=%fused_computation.64 | convolution fusion | flops 2157445120 | bytes 8388612 | tf_op jit(solution)/shard_map/dot_general | solution.py:154
  349.2 4.6 %add_convert_fusion = bf16[512,1024]{1,0:T(8,128)(2,1)S(1)} fusion(bf16[512,1024]{1,0:T(8,128)(2,1)S(1)} %collective-permute-done.23, bf16[4,512,2048]{2,1,0:T(8,128)(2,1)} %bitcast.12, s32[]{:T(128)S(6)} %select_n.302, bf16[1024,1024]{1,0:T(8,128)(2,1)} %collective-permute-done.16, bf16[1024,1024]{1,0:T(8,128)(2,1)S(1)} %copy-done.7), kind=kOutput, calls=%fused_computation.62 | convolution fusion | flops 2157445120 | bytes 8388612 | tf_op jit(solution)/shard_map/dot_general | solution.py:154
  353.8 1.3 collective-permute-start.25
  355.1 5.3 %collective-permute-start.24 = (bf16[512,1024]{1,0:T(8,128)(2,1)S(1)}, bf16[512,1024]{1,0:T(8,128)(2,1)S(1)}, u32[]{:S(2)}, u32[]{:S(2)}) collective-permute-start(bf16[512,1024]{1,0:T(8,128)(2,1)S(1)} %add_convert_fusion.1), channel_id=1, source_target_pairs={{0,8},{4,12},{8,16},{12,20},{16,24},{20,28},{1,9},{5,13},{9,17},{1... | collective-permute-start | bytes 3145736 | tf_op jit(solution)/shard_map/ppermute | solution.py:160
  360.5 6.6 %collective-permute-done.19 = bf16[512,1024]{1,0:T(8,128)(2,1)S(1)} collective-permute-done((bf16[512,1024]{1,0:T(8,128)(2,1)S(1)}, bf16[512,1024]{1,0:T(8,128)(2,1)S(1)}, u32[]{:S(2)}, u32[]{:S(2)}) %collective-permute-start.19) | collective-permute-done | bytes 1048608 | tf_op jit(solution)/shard_map/ppermute | solution.py:160
  367.6 4.6 %fusion.18 = f32[512,1024]{1,0:T(8,128)S(1)} fusion(bf16[4,512,2048]{2,1,0:T(8,128)(2,1)} %bitcast.12, s32[]{:T(128)S(6)} %select_n.303, bf16[1024,1024]{1,0:T(8,128)(2,1)} %collective-permute-done.16, bf16[1024,1024]{1,0:T(8,128)(2,1)S(1)} %copy-done.7), kind=kOutput, calls=%fused_computation.30 | convolution fusion | flops 2155872256 | bytes 8388612 | tf_op jit(solution)/shard_map/dot_general | solution.py:154
  372.1 6.9 %collective-permute-done.25 = bf16[512,1024]{1,0:T(8,128)(2,1)S(1)} collective-permute-done((bf16[512,1024]{1,0:T(8,128)(2,1)S(1)}, bf16[512,1024]{1,0:T(8,128)(2,1)S(1)}, u32[]{:S(2)}, u32[]{:S(2)}) %collective-permute-start.25) | collective-permute-done | bytes 1048608 | tf_op jit(solution)/shard_map/ppermute | solution.py:160
  379.1 9.2 %collective-permute-done.24 = bf16[512,1024]{1,0:T(8,128)(2,1)S(1)} collective-permute-done((bf16[512,1024]{1,0:T(8,128)(2,1)S(1)}, bf16[512,1024]{1,0:T(8,128)(2,1)S(1)}, u32[]{:S(2)}, u32[]{:S(2)}) %collective-permute-start.24) | collective-permute-done | bytes 1048608 | tf_op jit(solution)/shard_map/ppermute | solution.py:160
  388.8 1.3 copy-done.2
  390.1 4.4 %collective-permute-start.26 = (f32[3,2,1024]{2,1,0:T(2,128)S(1)}, f32[3,2,1024]{2,1,0:T(2,128)S(1)}, u32[]{:S(2)}, u32[]{:S(2)}) collective-permute-start(f32[3,2,1024]{2,1,0:T(2,128)S(1)} %pad_maximum_fusion.6), channel_id=1, source_target_pairs={{0,8},{4,12},{8,16},{12,20},{16,24},{20,28},{1,9},{5,13},{9,17},{1... | collective-permute-start | bytes 73736 | tf_op jit(solution)/shard_map/ppermute | solution.py:88
  394.6 1.4 collective-permute-done.26
  396.0 6.5 %fusion.10 = f32[64,8,8,128]{3,1,2,0:T(8,128)S(1)} fusion(f32[2,1024]{1,0:T(2,128)S(1)} %get-tuple-element.84, f32[512,1024]{1,0:T(8,128)} %copy-done.2, f32[2,1024]{1,0:T(2,128)S(1)} %get-tuple-element.85, f32[512,1024]{1,0:T(8,128)} %copy-done.1, f32[1024]{0:T(1024)S(1)} %bitcast.167, f32[1024]{0:T(1024)S(1)} %bitcast.168, f32[1024]{0:T(1024)S(1)} %bitcast.169, ...), kind=kLoop, calls=%fused_computation.19 | loop fusion | flops 7864320 | bytes 6332416
  402.9 2.4 shard_map.64
  405.3 1.3 collective-permute-start.29
  406.6 3.0 collective-permute-start.28
  409.7 1.8 collective-permute-start.27
  413.5 5.2 %shard_map.65 = f32[512,8,128]{2,1,0:T(8,128)S(1)} custom-call(f32[512,8,128]{2,1,0:T(8,128)S(1)} %bitcast.159, f32[512,8,128]{2,1,0:T(8,128)S(1)} %bitcast.160, f32[16,8,128]{2,1,0:T(8,128)S(1)} %bitcast.162, f32[16,8,128]{2,1,0:T(8,128)S(1)} %bitcast.163, f32[8,128]{1,0:T(8,128)S(1)} %dynamic-slice_bitcast_fusion.8.skip_ref, ...), custom_call_target="tpu_custom_call" | custom-call | tf_op jit(solution)/shard_map/pallas_call | solution.py:213
  419.3 1.7 collective-permute-start.30
  421.2 8.8 %collective-permute-done.30 = bf16[256,1024]{1,0:T(8,128)(2,1)S(1)} collective-permute-done((bf16[256,1024]{1,0:T(8,128)(2,1)S(1)}, bf16[256,1024]{1,0:T(8,128)(2,1)S(1)}, u32[]{:S(2)}, u32[]{:S(2)}) %collective-permute-start.30) | collective-permute-done | bytes 524320 | tf_op jit(solution)/shard_map/ppermute | solution.py:94
  (87 shorter events, 14.9 us)
Async XLA Ops:
  0.0 394.5 %copy-start = (f32[2048]{0:T(1024)S(1)}, f32[2048]{0:T(1024)}, u32[]{:S(2)}) copy-start(f32[2048]{0:T(1024)} %param.11) | copy-start | bytes 24580
  0.0 11.6 %collective-permute-start = (bf16[256,2048]{1,0:T(8,128)(2,1)}, bf16[256,2048]{1,0:T(8,128)(2,1)S(1)}, u32[]{:S(2)}, u32[]{:S(2)}) collective-permute-start(bf16[256,2048]{1,0:T(8,128)(2,1)} %param.6), channel_id=1, source_target_pairs={{0,0},{1,8},{2,16},{3,24},{4,4},{5,12},{6,20},{7,28},{8,2},{9,10},... | collective-permute-start | bytes 3145736 | tf_op jit(solution)/shard_map/ppermute | solution.py:111
  11.7 61.6 %collective-permute-start.4 = (bf16[1024,1024]{1,0:T(8,128)(2,1)}, bf16[1024,1024]{1,0:T(8,128)(2,1)}, u32[]{:S(2)}, u32[]{:S(2)}) collective-permute-start(bf16[1024,1024]{1,0:T(8,128)(2,1)} %get-tuple-element.31), channel_id=1, source_target_pairs={{0,4},{4,0},{8,12},{12,8},{16,20},{20,16},{24,28},{28,24},{1,5},{5... | collective-permute-start | bytes 6291464 | tf_op jit(solution)/shard_map/ppermute | solution.py:94
  20.6 45.9 %collective-permute-start.2 = (bf16[256,2048]{1,0:T(8,128)(2,1)S(1)}, bf16[256,2048]{1,0:T(8,128)(2,1)}, u32[]{:S(2)}, u32[]{:S(2)}) collective-permute-start(bf16[256,2048]{1,0:T(8,128)(2,1)S(1)} %get-tuple-element.56), channel_id=1, source_target_pairs={{0,2},{1,3},{2,0},{3,1},{4,6},{5,7},{6,4},{7,5},{8,10},{9,11},{10,... | collective-permute-start | bytes 3145736 | tf_op jit(solution)/shard_map/ppermute | solution.py:126
  39.2 33.6 %collective-permute-start.5 = (bf16[256,2048]{1,0:T(8,128)(2,1)S(1)}, bf16[256,2048]{1,0:T(8,128)(2,1)S(1)}, u32[]{:S(2)}, u32[]{:S(2)}) collective-permute-start(bf16[256,2048]{1,0:T(8,128)(2,1)S(1)} %collective-permute-done), channel_id=1, source_target_pairs={{0,4},{4,0},{8,12},{12,8},{16,20},{20,16},{24,28},{28,24},{1,5},{5... | collective-permute-start | bytes 3145736 | tf_op jit(solution)/shard_map/ppermute | solution.py:94
  39.8 63.7 %collective-permute-start.1 = (bf16[256,2048]{1,0:T(8,128)(2,1)S(1)}, bf16[256,2048]{1,0:T(8,128)(2,1)}, u32[]{:S(2)}, u32[]{:S(2)}) collective-permute-start(bf16[256,2048]{1,0:T(8,128)(2,1)S(1)} %get-tuple-element.56), channel_id=1, source_target_pairs={{0,1},{1,0},{2,3},{3,2},{4,5},{5,4},{6,7},{7,6},{8,9},{9,8},{10,11... | collective-permute-start | bytes 3145736 | tf_op jit(solution)/shard_map/ppermute | solution.py:129
  66.5 43.3 %collective-permute-start.3 = (bf16[256,2048]{1,0:T(8,128)(2,1)}, bf16[256,2048]{1,0:T(8,128)(2,1)S(1)}, u32[]{:S(2)}, u32[]{:S(2)}) collective-permute-start(bf16[256,2048]{1,0:T(8,128)(2,1)} %collective-permute-done.2), channel_id=1, source_target_pairs={{0,1},{1,0},{2,3},{3,2},{4,5},{5,4},{6,7},{7,6},{8,9},{9,8},{10,11... | collective-permute-start | bytes 3145736 | tf_op jit(solution)/shard_map/ppermute | solution.py:129
  73.3 53.6 %collective-permute-start.7 = (bf16[256,2048]{1,0:T(8,128)(2,1)S(1)}, bf16[256,2048]{1,0:T(8,128)(2,1)S(1)}, u32[]{:S(2)}, u32[]{:S(2)}) collective-permute-start(bf16[256,2048]{1,0:T(8,128)(2,1)S(1)} %maximum_select_fusion.1), channel_id=1, source_target_pairs={{0,2},{1,3},{2,0},{3,1},{4,6},{5,7},{6,4},{7,5},{8,10},{9,11},{10,... | collective-permute-start | bytes 3145736 | tf_op jit(solution)/shard_map/ppermute | solution.py:126
  103.5 4.8 %copy-start.6 = (bf16[1024,1024]{1,0:T(8,128)(2,1)S(1)}, bf16[1024,1024]{1,0:T(8,128)(2,1)}, u32[]{:S(2)}) copy-start(bf16[1024,1024]{1,0:T(8,128)(2,1)} %get-tuple-element.33) | copy-start | bytes 6291460
  106.0 22.0 %collective-permute-start.6 = (bf16[256,2048]{1,0:T(8,128)(2,1)S(1)}, bf16[256,2048]{1,0:T(8,128)(2,1)S(1)}, u32[]{:S(2)}, u32[]{:S(2)}) collective-permute-start(bf16[256,2048]{1,0:T(8,128)(2,1)S(1)} %maximum_select_fusion.1), channel_id=1, source_target_pairs={{0,1},{1,0},{2,3},{3,2},{4,5},{5,4},{6,7},{7,6},{8,9},{9,8},{10,11... | collective-permute-start | bytes 3145736 | tf_op jit(solution)/shard_map/ppermute | solution.py:129
  108.3 48.0 %collective-permute-start.9 = (bf16[1024,1024]{1,0:T(8,128)(2,1)S(1)}, bf16[1024,1024]{1,0:T(8,128)(2,1)S(1)}, u32[]{:S(2)}, u32[]{:S(2)}) collective-permute-start(bf16[1024,1024]{1,0:T(8,128)(2,1)S(1)} %copy-done.6), channel_id=1, source_target_pairs={{0,4},{4,0},{8,12},{12,8},{16,20},{20,16},{24,28},{28,24},{1,5},{5... | collective-permute-start | bytes 6291464 | tf_op jit(solution)/shard_map/ppermute | solution.py:94
  126.9 3.2 collective-permute-start.8
  129.1 27.3 %copy-start.4 = (bf16[1024,1024]{1,0:T(8,128)(2,1)S(1)}, bf16[1024,1024]{1,0:T(8,128)(2,1)}, u32[]{:S(2)}) copy-start(bf16[1024,1024]{1,0:T(8,128)(2,1)} %get-tuple-element.60) | copy-start | bytes 6291460
  156.3 5.8 %copy-start.12 = (bf16[1024,1024]{1,0:T(8,128)(2,1)}, bf16[1024,1024]{1,0:T(8,128)(2,1)S(1)}, u32[]{:S(2)}) copy-start(bf16[1024,1024]{1,0:T(8,128)(2,1)S(1)} %collective-permute-done.9) | copy-start | bytes 6291460
  156.3 32.2 %copy-start.3 = (bf16[1024,1024]{1,0:T(8,128)(2,1)S(1)}, bf16[1024,1024]{1,0:T(8,128)(2,1)}, u32[]{:S(2)}) copy-start(bf16[1024,1024]{1,0:T(8,128)(2,1)} %get-tuple-element.64) | copy-start | bytes 6291460
  162.1 47.8 %collective-permute-start.10 = (bf16[512,1024]{1,0:T(8,128)(2,1)}, bf16[512,1024]{1,0:T(8,128)(2,1)}, u32[]{:S(2)}, u32[]{:S(2)}) collective-permute-start(bf16[512,1024]{1,0:T(8,128)(2,1)} %fusion.63), channel_id=1, source_target_pairs={{0,8},{4,12},{24,16},{28,20},{1,9},{5,13},{25,17},{29,21},{2,10},{... | collective-permute-start | bytes 3145736 | tf_op jit(solution)/shard_map/ppermute | solution.py:160
  187.0 50.2 %collective-permute-start.16 = (bf16[1024,1024]{1,0:T(8,128)(2,1)}, bf16[1024,1024]{1,0:T(8,128)(2,1)}, u32[]{:S(2)}, u32[]{:S(2)}) collective-permute-start(bf16[1024,1024]{1,0:T(8,128)(2,1)} %get-tuple-element.42), channel_id=1, source_target_pairs={{0,4},{4,0},{8,12},{12,8},{16,20},{20,16},{24,28},{28,24},{1,5},{5... | collective-permute-start | bytes 6291464 | tf_op jit(solution)/shard_map/ppermute | solution.py:94
  188.5 7.8 %copy-start.11 = (bf16[3,3,2048]{2,1,0:T(4,128)(2,1)S(1)}, bf16[3,3,2048]{2,1,0:T(4,128)(2,1)}, u32[]{:S(2)}) copy-start(bf16[3,3,2048]{2,1,0:T(4,128)(2,1)} %param.8) | copy-start | bytes 110596
  194.1 38.2 %collective-permute-start.15 = (bf16[512,1024]{1,0:T(8,128)(2,1)}, bf16[512,1024]{1,0:T(8,128)(2,1)}, u32[]{:S(2)}, u32[]{:S(2)}) collective-permute-start(bf16[512,1024]{1,0:T(8,128)(2,1)} %fusion.66), channel_id=1, source_target_pairs={{0,8},{4,12},{24,16},{28,20},{1,9},{5,13},{25,17},{29,21},{2,10},{... | collective-permute-start | bytes 3145736 | tf_op jit(solution)/shard_map/ppermute | solution.py:160
  196.4 23.3 %copy-start.9 = (f32[2048,16]{0,1:T(8,128)S(1)}, f32[2048,16]{0,1:T(8,128)}, u32[]{:S(2)}) copy-start(f32[2048,16]{0,1:T(8,128)} %param.9) | copy-start | bytes 393220
  196.4 23.3 %copy-start.10 = (f32[2048,16]{0,1:T(8,128)S(1)}, f32[2048,16]{0,1:T(8,128)}, u32[]{:S(2)}) copy-start(f32[2048,16]{0,1:T(8,128)} %param.10) | copy-start | bytes 393220
  215.3 39.4 %collective-permute-start.11 = (bf16[512,1024]{1,0:T(8,128)(2,1)S(1)}, bf16[512,1024]{1,0:T(8,128)(2,1)S(1)}, u32[]{:S(2)}, u32[]{:S(2)}) collective-permute-start(bf16[512,1024]{1,0:T(8,128)(2,1)S(1)} %add_convert_fusion.8), channel_id=1, source_target_pairs={{0,8},{4,12},{8,16},{12,20},{1,9},{5,13},{9,17},{13,21},{2,10},{6,... | collective-permute-start | bytes 3145736 | tf_op jit(solution)/shard_map/ppermute | solution.py:160
  219.8 22.6 %copy-start.7 = (bf16[1024,1024]{1,0:T(8,128)(2,1)S(1)}, bf16[1024,1024]{1,0:T(8,128)(2,1)}, u32[]{:S(2)}) copy-start(bf16[1024,1024]{1,0:T(8,128)(2,1)} %get-tuple-element.62) | copy-start | bytes 6291460
  219.9 38.8 %collective-permute-start.12 = (bf16[512,1024]{1,0:T(8,128)(2,1)S(1)}, bf16[512,1024]{1,0:T(8,128)(2,1)S(1)}, u32[]{:S(2)}, u32[]{:S(2)}) collective-permute-start(bf16[512,1024]{1,0:T(8,128)(2,1)S(1)} %add_convert_fusion.8), channel_id=1, source_target_pairs={{24,16},{28,20},{16,8},{20,12},{25,17},{29,21},{17,9},{21,13},{26,... | collective-permute-start | bytes 3145736 | tf_op jit(solution)/shard_map/ppermute | solution.py:160
  237.2 71.5 %collective-permute-start.17 = (bf16[512,1024]{1,0:T(8,128)(2,1)S(1)}, bf16[512,1024]{1,0:T(8,128)(2,1)S(1)}, u32[]{:S(2)}, u32[]{:S(2)}) collective-permute-start(bf16[512,1024]{1,0:T(8,128)(2,1)S(1)} %add_convert_fusion.5), channel_id=1, source_target_pairs={{0,8},{4,12},{8,16},{12,20},{1,9},{5,13},{9,17},{13,21},{2,10},{6,... | collective-permute-start | bytes 3145736 | tf_op jit(solution)/shard_map/ppermute | solution.py:160
  241.7 72.6 %collective-permute-start.18 = (bf16[512,1024]{1,0:T(8,128)(2,1)S(1)}, bf16[512,1024]{1,0:T(8,128)(2,1)S(1)}, u32[]{:S(2)}, u32[]{:S(2)}) collective-permute-start(bf16[512,1024]{1,0:T(8,128)(2,1)S(1)} %add_convert_fusion.5), channel_id=1, source_target_pairs={{24,16},{28,20},{16,8},{20,12},{25,17},{29,21},{17,9},{21,13},{26,... | collective-permute-start | bytes 3145736 | tf_op jit(solution)/shard_map/ppermute | solution.py:160
  242.4 12.3 %copy-start.5 = (bf16[1024,1024]{1,0:T(8,128)(2,1)S(1)}, bf16[1024,1024]{1,0:T(8,128)(2,1)}, u32[]{:S(2)}) copy-start(bf16[1024,1024]{1,0:T(8,128)(2,1)} %get-tuple-element.60) | copy-start | bytes 6291460
  242.4 12.3 %copy-start.13 = (bf16[1024,1024]{1,0:T(8,128)(2,1)S(1)}, bf16[1024,1024]{1,0:T(8,128)(2,1)}, u32[]{:S(2)}) copy-start(bf16[1024,1024]{1,0:T(8,128)(2,1)} %copy-done.12) | copy-start | bytes 6291460
  247.2 52.5 %collective-permute-start.21 = (bf16[512,1024]{1,0:T(8,128)(2,1)S(1)}, bf16[512,1024]{1,0:T(8,128)(2,1)S(1)}, u32[]{:S(2)}, u32[]{:S(2)}) collective-permute-start(bf16[512,1024]{1,0:T(8,128)(2,1)S(1)} %fusion.69), channel_id=1, source_target_pairs={{0,8},{4,12},{24,16},{28,20},{1,9},{5,13},{25,17},{29,21},{2,10},{... | collective-permute-start | bytes 3145736 | tf_op jit(solution)/shard_map/ppermute | solution.py:160
  262.7 62.1 %collective-permute-start.14 = (bf16[512,1024]{1,0:T(8,128)(2,1)S(1)}, bf16[512,1024]{1,0:T(8,128)(2,1)S(1)}, u32[]{:S(2)}, u32[]{:S(2)}) collective-permute-start(bf16[512,1024]{1,0:T(8,128)(2,1)S(1)} %add_convert_fusion.6), channel_id=1, source_target_pairs={{24,16},{28,20},{16,8},{20,12},{8,0},{12,4},{25,17},{29,21},{17,9}... | collective-permute-start | bytes 3145736 | tf_op jit(solution)/shard_map/ppermute | solution.py:160
  264.0 65.4 %collective-permute-start.13 = (bf16[512,1024]{1,0:T(8,128)(2,1)S(1)}, bf16[512,1024]{1,0:T(8,128)(2,1)S(1)}, u32[]{:S(2)}, u32[]{:S(2)}) collective-permute-start(bf16[512,1024]{1,0:T(8,128)(2,1)S(1)} %add_convert_fusion.7), channel_id=1, source_target_pairs={{0,8},{4,12},{8,16},{12,20},{16,24},{20,28},{1,9},{5,13},{9,17},{1... | collective-permute-start | bytes 3145736 | tf_op jit(solution)/shard_map/ppermute | solution.py:160
  304.2 40.4 %collective-permute-start.22 = (bf16[512,1024]{1,0:T(8,128)(2,1)S(1)}, bf16[512,1024]{1,0:T(8,128)(2,1)S(1)}, u32[]{:S(2)}, u32[]{:S(2)}) collective-permute-start(bf16[512,1024]{1,0:T(8,128)(2,1)S(1)} %add_convert_fusion.2), channel_id=1, source_target_pairs={{0,8},{4,12},{8,16},{12,20},{1,9},{5,13},{9,17},{13,21},{2,10},{6,... | collective-permute-start | bytes 3145736 | tf_op jit(solution)/shard_map/ppermute | solution.py:160
  308.7 40.5 %collective-permute-start.23 = (bf16[512,1024]{1,0:T(8,128)(2,1)S(1)}, bf16[512,1024]{1,0:T(8,128)(2,1)S(1)}, u32[]{:S(2)}, u32[]{:S(2)}) collective-permute-start(bf16[512,1024]{1,0:T(8,128)(2,1)S(1)} %add_convert_fusion.2), channel_id=1, source_target_pairs={{24,16},{28,20},{16,8},{20,12},{25,17},{29,21},{17,9},{21,13},{26,... | collective-permute-start | bytes 3145736 | tf_op jit(solution)/shard_map/ppermute | solution.py:160
  318.9 41.6 %collective-permute-start.20 = (bf16[512,1024]{1,0:T(8,128)(2,1)S(1)}, bf16[512,1024]{1,0:T(8,128)(2,1)S(1)}, u32[]{:S(2)}, u32[]{:S(2)}) collective-permute-start(bf16[512,1024]{1,0:T(8,128)(2,1)S(1)} %add_convert_fusion.3), channel_id=1, source_target_pairs={{24,16},{28,20},{16,8},{20,12},{8,0},{12,4},{25,17},{29,21},{17,9}... | collective-permute-start | bytes 3145736 | tf_op jit(solution)/shard_map/ppermute | solution.py:160
  324.8 42.3 %collective-permute-start.19 = (bf16[512,1024]{1,0:T(8,128)(2,1)S(1)}, bf16[512,1024]{1,0:T(8,128)(2,1)S(1)}, u32[]{:S(2)}, u32[]{:S(2)}) collective-permute-start(bf16[512,1024]{1,0:T(8,128)(2,1)S(1)} %add_convert_fusion.4), channel_id=1, source_target_pairs={{0,8},{4,12},{8,16},{12,20},{16,24},{20,28},{1,9},{5,13},{9,17},{1... | collective-permute-start | bytes 3145736 | tf_op jit(solution)/shard_map/ppermute | solution.py:160
  330.0 30.5 %copy-start.1 = (f32[512,1024]{1,0:T(8,128)}, f32[512,1024]{1,0:T(8,128)S(1)}, u32[]{:S(2)}) copy-start(f32[512,1024]{1,0:T(8,128)S(1)} %convert_add_fusion.2) | copy-start | bytes 6291460
  353.8 25.3 %collective-permute-start.25 = (bf16[512,1024]{1,0:T(8,128)(2,1)S(1)}, bf16[512,1024]{1,0:T(8,128)(2,1)S(1)}, u32[]{:S(2)}, u32[]{:S(2)}) collective-permute-start(bf16[512,1024]{1,0:T(8,128)(2,1)S(1)} %add_convert_fusion), channel_id=1, source_target_pairs={{24,16},{28,20},{16,8},{20,12},{8,0},{12,4},{25,17},{29,21},{17,9}... | collective-permute-start | bytes 3145736 | tf_op jit(solution)/shard_map/ppermute | solution.py:160
  355.1 33.2 %collective-permute-start.24 = (bf16[512,1024]{1,0:T(8,128)(2,1)S(1)}, bf16[512,1024]{1,0:T(8,128)(2,1)S(1)}, u32[]{:S(2)}, u32[]{:S(2)}) collective-permute-start(bf16[512,1024]{1,0:T(8,128)(2,1)S(1)} %add_convert_fusion.1), channel_id=1, source_target_pairs={{0,8},{4,12},{8,16},{12,20},{16,24},{20,28},{1,9},{5,13},{9,17},{1... | collective-permute-start | bytes 3145736 | tf_op jit(solution)/shard_map/ppermute | solution.py:160
  388.8 1.3 copy-start.2
  390.1 5.9 %collective-permute-start.26 = (f32[3,2,1024]{2,1,0:T(2,128)S(1)}, f32[3,2,1024]{2,1,0:T(2,128)S(1)}, u32[]{:S(2)}, u32[]{:S(2)}) collective-permute-start(f32[3,2,1024]{2,1,0:T(2,128)S(1)} %pad_maximum_fusion.6), channel_id=1, source_target_pairs={{0,8},{4,12},{8,16},{12,20},{16,24},{20,28},{1,9},{5,13},{9,17},{1... | collective-permute-start | bytes 73736 | tf_op jit(solution)/shard_map/ppermute | solution.py:88
  405.3 7.3 %collective-permute-start.29 = (f32[16,8,128]{2,1,0:T(8,128)S(1)}, f32[16,8,128]{2,1,0:T(8,128)S(1)}, u32[]{:S(2)}, u32[]{:S(2)}) collective-permute-start(f32[16,8,128]{2,1,0:T(8,128)S(1)} %shard_map.64), channel_id=1, source_target_pairs={{0,24},{4,28},{1,25},{5,29},{2,26},{6,30},{3,27},{7,31}} | collective-permute-start | bytes 196616 | tf_op jit(solution)/shard_map/ppermute | solution.py:88
  406.6 6.0 %collective-permute-start.28 = (f32[16,8,128]{2,1,0:T(8,128)S(1)}, f32[16,8,128]{2,1,0:T(8,128)S(1)}, u32[]{:S(2)}, u32[]{:S(2)}) collective-permute-start(f32[16,8,128]{2,1,0:T(8,128)S(1)} %shard_map.64), channel_id=1, source_target_pairs={{0,16},{4,20},{8,24},{12,28},{1,17},{5,21},{9,25},{13,29},{2,18},{... | collective-permute-start | bytes 196616 | tf_op jit(solution)/shard_map/ppermute | solution.py:88
  409.7 3.7 collective-permute-start.27
  419.3 10.7 %collective-permute-start.30 = (bf16[256,1024]{1,0:T(8,128)(2,1)S(1)}, bf16[256,1024]{1,0:T(8,128)(2,1)S(1)}, u32[]{:S(2)}, u32[]{:S(2)}) collective-permute-start(bf16[256,1024]{1,0:T(8,128)(2,1)S(1)} %dynamic-slice_bitcast_fusion.6), channel_id=1, source_target_pairs={{0,4},{4,0},{8,12},{12,8},{16,20},{20,16},{24,28},{28,24},{1,5},{5... | collective-permute-start | bytes 1572872 | tf_op jit(solution)/shard_map/ppermute | solution.py:94
  421.2 8.8 %copy-start.8 = (bf16[256,2048]{1,0:T(8,128)(2,1)}, bf16[256,2048]{1,0:T(8,128)(2,1)S(1)}, u32[]{:S(2)}) copy-start(bf16[256,2048]{1,0:T(8,128)(2,1)S(1)} %bitcast_dynamic-update-slice_fusion.8) | copy-start | bytes 3145732
